TPU v7x, 32 devices: a whole 2x2x4 slice. The times are simulated.
32 devices in a mesh: groups: 2 (over y), seq: 16 (over z, x, core).
Axes of the slice: x: 2, y: 2, z: 4, core: 2. Of those that a mesh axis runs over, the one named last changes fastest.
Arguments:
- hidden: bfloat16 [4, 4, 8192], P('groups', None, 'seq'), parts along dimension 0, may hold values from -1200 to 1200
- norm_gain: bfloat16 [8192], P('seq'), may hold values from 0.099609375 to 1.8984375
- q_weight: bfloat16 [8192, 8192], P('seq'), may hold values from -0.0625 to 0.0625
- kv_weight: bfloat16 [8192, 2048], P('seq'), may hold values from -0.0625 to 0.0625
- out_weight: bfloat16 [8192, 8192], P('seq'), may hold values from -0.09375 to 0.09375
- head_kind: int32 [8], replicated, may hold values from 0 to 1, as said below
- ret_keys: bfloat16 [4, 4, 32768, 128], P('groups', None, 'seq'), parts along dimension 0, may hold values from -600 to 600
- ret_values: bfloat16 [4, 4, 32768, 128], P('groups', None, 'seq'), parts along dimension 0, may hold values from -8 to 8
- stream_keys: bfloat16 [4, 4, 2048, 128], P('groups', None, 'seq'), parts along dimension 0, may hold values from -600 to 600
- stream_values: bfloat16 [4, 4, 2048, 128], P('groups', None, 'seq'), parts along dimension 0, may hold values from -8 to 8
- cache_len: int32 [4], P('groups'), parts along dimension 0, may hold values from 1 to 32768, as said below
- sink_len: int32 [4], P('groups'), parts along dimension 0, may hold values from 1 to 128, as said below
- window_len: int32 [4], P('groups'), parts along dimension 0, may hold values from 1 to 1920, as said below
Outputs:
- layer_output: bfloat16 [4, 4, 8192], P('groups', None, 'seq'), parts along dimension 0
- new_entries: bfloat16 [4, 4, 2048], P('groups'), parts along dimension 0
There are 2 independent parts, one for each index of `groups`. A program takes and returns all parts, laid end to end along the dimension named above; an argument that names none is the same for every part. Nothing has to cross between parts.
Inputs may be any that keep to these rules, and one draw needn't show every extreme that they name: `head_kind`: exactly 4 of the 8 entries are 1, the others 0. `cache_len`: in every draw some request has all 32768 positions filled. `sink_len`: in every draw some request holds 128 sink tokens. `window_len`: in every draw some request holds 1920 recent tokens.
All inputs are finite; a program needn't handle non-finite values.
Results may differ from a plain program's by a relative error of at most 0.0075.
The roundings to bfloat16 on the way count: a program that leaves them out, or rounds other values in their place, can miss the bound.
Values may be sent and summed in bfloat16 or wider, within the bound.
A program may use at most 128 MiB of HBM per device.

v0:
```python
import jax
import jax.numpy as jnp
from jax import lax
from jax.sharding import PartitionSpec as P

SINK_CAP = 128


epsilon = 1e-05
floor_score = -1e30


def joined(part, axis, combine):
    gathered = jax.tree.map(lambda a: lax.all_gather(a, axis), part)

    def take(source):
        return jax.tree.map(lambda a: lax.dynamic_index_in_dim(a, source, 0, False), gathered)

    return lax.fori_loop(
        1, lax.axis_size(axis), lambda source, state: combine(state, take(source)), take(0)
    )


def block_stats(queries, cache_keys, cache_values, visible, score_scale):
    scores = (
        jnp.einsum("bhqd,bhld->bhql", queries, cache_keys, preferred_element_type=jnp.float32)
        * score_scale
    )
    scores = jnp.where(visible, scores, floor_score)
    peak_score = jnp.max(scores, axis=-1)
    weights = jnp.where(visible, jnp.exp(scores - peak_score[..., None]), 0.0)
    weight_total = jnp.sum(weights, axis=-1)
    block_out = jnp.einsum(
        "bhql,bhld->bhqd",
        weights.astype(jnp.bfloat16),
        cache_values,
        preferred_element_type=jnp.float32,
    )
    return (peak_score, weight_total, block_out)


def spread_rows(values_in, selector):
    return jnp.einsum("brq,gr->bgq", values_in, selector, precision=lax.Precision.HIGHEST)


def spread_vectors(values_in, selector):
    return jnp.einsum("brqd,gr->bgqd", values_in, selector, precision=lax.Precision.HIGHEST)


def join_parts(first_part, second_part):
    top_score = jnp.maximum(first_part[0], second_part[0])
    left_factor = jnp.exp(first_part[0] - top_score)
    right_factor = jnp.exp(second_part[0] - top_score)
    joined_total = first_part[1] * left_factor + second_part[1] * right_factor
    joined_out = first_part[2] * left_factor[..., None] + second_part[2] * right_factor[..., None]
    return (top_score, joined_total, joined_out)


def per_device(
    hidden,
    norm_gain,
    q_weight,
    kv_weight,
    out_weight,
    head_kind,
    ret_keys,
    ret_values,
    stream_keys,
    stream_values,
    cache_len,
    sink_len,
    window_len,
):
    requests, drafts, local_width = hidden.shape
    kv_heads = head_kind.shape[0]
    head_dim = ret_keys.shape[3]
    retrieval = ret_keys.shape[1]
    running = stream_keys.shape[1]
    head_count = q_weight.shape[1] // head_dim
    group_size = head_count // kv_heads
    query_rows = drafts * group_size
    devices = lax.axis_size("seq")
    position = lax.axis_index("seq")
    tokens = requests * drafts
    hidden32 = hidden.astype(jnp.float32)
    squares = lax.psum(jnp.sum(hidden32 * hidden32, axis=-1), "seq")
    inverse = lax.rsqrt(squares / (local_width * devices) + epsilon)
    normed = (hidden32 * inverse[..., None] * norm_gain.astype(jnp.float32)).astype(jnp.bfloat16)
    flat_rows = normed.reshape(tokens, local_width)
    part_query = jnp.dot(flat_rows, q_weight, preferred_element_type=jnp.float32)
    part_fresh = jnp.dot(flat_rows, kv_weight, preferred_element_type=jnp.float32)
    whole_query, whole_fresh = lax.psum((part_query, part_fresh), "seq")
    queries = whole_query.astype(jnp.bfloat16)
    new_entries = whole_fresh.astype(jnp.bfloat16)
    grouped = (
        queries.reshape(requests, drafts, kv_heads, group_size, head_dim)
        .transpose(0, 2, 1, 3, 4)
        .reshape(requests, kv_heads, query_rows, head_dim)
    )
    fresh_split = new_entries.reshape(requests, drafts, 2, kv_heads, head_dim)
    new_keys = fresh_split[:, :, 0].transpose(0, 2, 1, 3)
    new_values = fresh_split[:, :, 1].transpose(0, 2, 1, 3)
    kind_flag = head_kind == 1
    rank_ret = jnp.cumsum(head_kind) - 1
    rank_str = jnp.cumsum(1 - head_kind) - 1
    select_ret = (
        kind_flag[:, None] & (rank_ret[:, None] == jnp.arange(retrieval)[None, :])
    ).astype(jnp.float32)
    select_str = (
        jnp.logical_not(kind_flag)[:, None] & (rank_str[:, None] == jnp.arange(running)[None, :])
    ).astype(jnp.float32)
    ret_queries = jnp.einsum(
        "bgqd,gr->brqd",
        grouped,
        select_ret.astype(jnp.bfloat16),
        preferred_element_type=jnp.float32,
    ).astype(jnp.bfloat16)
    str_queries = jnp.einsum(
        "bgqd,gr->brqd",
        grouped,
        select_str.astype(jnp.bfloat16),
        preferred_element_type=jnp.float32,
    ).astype(jnp.bfloat16)
    score_scale = head_dim ** (-0.5)
    cache_block = ret_keys.shape[2]
    cache_pos = position * cache_block + jnp.arange(cache_block)
    ret_visible = (cache_pos[None, :] < cache_len[:, None])[:, None, None, :]
    slot_block = stream_keys.shape[2]
    slot_pos = (position * slot_block + jnp.arange(slot_block))[None, :]
    sink_part = slot_pos < sink_len[:, None]
    recent_part = (slot_pos >= SINK_CAP) & (slot_pos < SINK_CAP + window_len[:, None])
    str_visible = (sink_part | recent_part)[:, None, None, :]
    ret_peak, ret_total, ret_out = block_stats(
        ret_queries, ret_keys, ret_values, ret_visible, score_scale
    )
    str_peak, str_total, str_out = block_stats(
        str_queries, stream_keys, stream_values, str_visible, score_scale
    )
    peak_all = spread_rows(ret_peak, select_ret) + spread_rows(str_peak, select_str)
    total_all = spread_rows(ret_total, select_ret) + spread_rows(str_total, select_str)
    out_all = spread_vectors(ret_out, select_ret) + spread_vectors(str_out, select_str)
    token_of_row = jnp.arange(query_rows) // group_size
    new_visible = jnp.arange(drafts)[None, :] <= token_of_row[:, None]
    new_peak, new_total, new_out = block_stats(
        grouped, new_keys, new_values, new_visible, score_scale
    )
    own_width = out_weight.shape[0]
    cache_peak, cache_total, cache_out = joined((peak_all, total_all, out_all), "seq", join_parts)
    top_score = jnp.maximum(cache_peak, new_peak)
    cache_factor = jnp.exp(cache_peak - top_score)
    new_factor = jnp.exp(new_peak - top_score)
    denominator = cache_total * cache_factor + new_total * new_factor
    attended = (
        cache_out * cache_factor[..., None] + new_out * new_factor[..., None]
    ) / denominator[..., None]
    attention = (
        attended.reshape(requests, kv_heads, drafts, group_size, head_dim)
        .transpose(0, 2, 1, 3, 4)
        .reshape(tokens, head_count * head_dim)
        .astype(jnp.bfloat16)
    )
    own_attention = lax.dynamic_slice_in_dim(attention, position * own_width, own_width, 1)
    own_output = lax.psum_scatter(
        lax.dot_general(
            out_weight, own_attention, (((0,), (1,)), ((), ())), preferred_element_type=jnp.float32
        ),
        "seq",
        scatter_dimension=0,
        tiled=True,
    )
    layer_output = own_output.T.reshape(requests, drafts, local_width).astype(jnp.bfloat16)
    return (layer_output, new_entries.reshape(requests, drafts, 2 * kv_heads * head_dim))


def solution(mesh):
    in_specs = (
        P("groups", None, "seq"),
        P("seq"),
        P("seq", None),
        P("seq", None),
        P("seq", None),
        P(),
        P("groups", None, "seq", None),
        P("groups", None, "seq", None),
        P("groups", None, "seq", None),
        P("groups", None, "seq", None),
        P("groups"),
        P("groups"),
        P("groups"),
    )
    out_specs = (P("groups", None, "seq"), P("groups", None, None))
    return jax.shard_map(
        per_device, mesh=mesh, in_specs=in_specs, out_specs=out_specs, check_vma=False
    )
```

profile of v0, /device:TPU:0, one launch (start us, length us, event | category | flops | bytes accessed | tf_op | source)
XLA Modules:
  0.0 258.2 jit_solution(16587945270876655756)
XLA Ops:
  7.2 0.0 copy-start
  7.2 0.0 all-gather.5.cloned.1.call-start
  7.3 0.8 subtract_bitcast_fusion
  8.0 0.7 fusion.65
  8.7 0.7 broadcast_add_fusion
  9.4 0.8 reduce-window.16
  10.2 0.2 reduce-window.17
  10.4 0.8 fusion.37
  11.2 34.9 %psum.21 = f32[2,4]{1,0:T(2,128)S(1)} all-reduce(f32[2,4]{1,0:T(2,128)S(1)} %fusion.37), channel_id=1, replica_groups=mesh['groups'=2,'seq'=16] {'seq'}, use_global_device_ids=true, to_apply=%region_2.0 | all-reduce | flops 8 | bytes 64 | tf_op jit(solution)/shard_map/psum | solution.py:86
  46.1 0.7 convert_element_type.72
  46.8 0.8 fusion.39
  47.6 0.4 fusion.74
  47.9 4.6 %fusion.73 = f32[8,8192]{1,0:T(8,128)S(1)} fusion(bf16[8,512]{1,0:T(8,128)(2,1)S(1)} %reshape.194, bf16[512,8192]{1,0:T(8,128)(2,1)} %param.17), kind=kOutput, calls=%fused_computation.113 | convolution fusion | flops 67108864 | bytes 8658944 | tf_op jit(solution)/shard_map/dot_general | solution.py:90
  52.5 60.7 %all-reduce.2 = (bf16[8,8192]{1,0:T(8,128)(2,1)S(1)}, bf16[8,2048]{1,0:T(8,128)(2,1)S(1)}) all-reduce(f32[8,8192]{1,0:T(8,128)S(1)} %fusion.73, f32[8,2048]{1,0:T(8,128)S(1)} %fusion.74), channel_id=1, replica_groups=mesh['groups'=2,'seq'=16] {'seq'}, use_global_device_ids=true, to_apply=%region_3.0 | all-reduce | flops 81920 | bytes 491520 | tf_op jit(solution)/shard_map/psum | solution.py:92
  113.3 0.2 fusion.13
  113.4 0.2 fusion.12
  113.6 0.1 broadcast_compare_fusion
  113.7 3.9 %fusion.70 = (f32[2,4,32]{2,1,0:T(4,128)S(1)}, f32[2,4,32,2048]{3,2,1,0:T(8,128)S(1)}) fusion(bf16[2,4,2048,128]{3,2,1,0:T(8,128)(2,1)} %param.21, bf16[2,4,32,128]{3,1,2,0:T(4,128)(2,1)S(1)} %fusion.12, pred[2,2048]{1,0:T(4,128)(4,1)S(1)} %broadcast_compare_fusion), kind=kOutput, calls=%fused_computation.110 | convolution fusion | flops 135790336 | bytes 6362112 | tf_op jit(solution)/shard_map/bhqd,bhld->bhql/dot_general | solution.py:26
  117.7 0.0 copy-start.6
  117.7 0.9 fusion.17
  118.6 0.4 copy-done.1
  119.0 0.3 fusion.24
  119.4 0.1 and_or_fusion
  119.4 0.3 fusion.71
  119.8 0.3 fusion.28
  120.0 0.4 fusion.8
  120.4 0.8 copy.31
  121.2 0.0 all-gather.5.cloned.1.call-update
  121.2 0.0 reduce-scatter.2.cloned.1.call-start
  121.3 0.2 fusion.27
  121.5 2.1 fusion.5
  123.6 0.2 fusion.53
  123.8 0.2 fusion.15
  124.0 17.7 %all-gather.1 = f32[32,8,32]{2,1,0:T(8,128)S(1)} all-gather(f32[2,8,32]{2,1,0:T(8,128)S(1)} %fusion.15), channel_id=3, replica_groups=mesh['groups'=2,'seq'=16] {'seq'}, dimensions={0}, use_global_device_ids=true | all-gather | bytes 34816 | tf_op jit(solution)/shard_map/all_gather | solution.py:14
  141.6 0.2 fusion.55
  141.8 0.2 fusion.16
  142.0 20.0 %all-gather = f32[32,8,32]{2,1,0:T(8,128)S(1)} all-gather(f32[2,8,32]{2,1,0:T(8,128)S(1)} %fusion.16), channel_id=2, replica_groups=mesh['groups'=2,'seq'=16] {'seq'}, dimensions={0}, use_global_device_ids=true | all-gather | bytes 34816 | tf_op jit(solution)/shard_map/all_gather | solution.py:14
  162.0 0.2 fusion.72
  162.3 7.9 %all-gather.5.cloned.1.call-done = f32[32,8,32,128]{3,2,1,0:T(8,128)} async-done(((f32[2,8,32,128]{3,2,1,0:T(8,128)}), f32[32,8,32,128]{3,2,1,0:T(8,128)}) %all-gather.5.cloned.1.call-update) | async-done | bytes 4194320 | tf_op jit(solution)/shard_map/all_gather | solution.py:14
  170.2 1.0 slice.16
  171.1 18.9 %while.19 = (s32[]{:T(128)}, f32[2,8,32]{2,1,0:T(8,128)S(1)}, f32[2,8,32]{2,1,0:T(8,128)S(1)}, f32[2,8,32,128]{3,2,1,0:T(8,128)S(1)}, f32[16,2,8,32]{3,2,1,0:T(8...) while((s32[]{:T(128)}, f32[2,8,32]{2,1,0:T(8,128)S(1)}, ...), condition=%wide.region_10.11_spmd, body=%wide.region_9.10_spmd.sunk | while | flops 199685 | bytes 807055 | solution.py:19
  171.2 1.2 fusion.93
  172.4 1.2 fusion.93
  173.7 1.2 fusion.93
  175.0 1.2 fusion.93
  176.2 1.2 fusion.93
  177.5 1.2 fusion.93
  178.8 1.2 fusion.93
  180.0 1.2 fusion.93
  181.3 1.2 fusion.93
  182.5 1.2 fusion.93
  183.8 1.2 fusion.93
  185.1 1.2 fusion.93
  186.3 1.2 fusion.93
  187.6 1.2 fusion.93
  188.9 1.2 fusion.93
  190.1 0.4 fusion.10
  190.5 0.1 convert_element_type.88
  190.6 5.3 %convolution_bitcast_fusion = f32[8192,8]{0,1:T(8,128)} fusion(bf16[512,8192]{1,0:T(8,128)(2,1)} %param.19, bf16[8,8192]{1,0:T(8,128)(2,1)S(1)} %convert_element_type.88, s32[]{:T(128)S(6)} %select_n.59), kind=kOutput, calls=%fused_computation.8 | convolution fusion | flops 67108864 | bytes 8658948 | tf_op jit(solution)/shard_map/dot_general | solution.py:164
  195.9 0.0 reduce-scatter.2.cloned.1.call-update
  195.9 0.6 reshape.199
  196.5 53.5 %reduce-scatter.2.cloned.1.call-done = f32[512,8]{0,1:T(8,128)} async-done(((f32[8192,8]{0,1:T(8,128)}), f32[512,8]{0,1:T(8,128)}) %reduce-scatter.2.cloned.1.call-update) | async-done | bytes 16400 | tf_op jit(solution)/shard_map/reduce_scatter | solution.py:163
  250.1 0.7 convert_bitcast_fusion.1
  250.8 0.6 convert_element_type.91
  (45 shorter events, 0.5 us)
Async XLA Ops:
  7.2 40.4 %copy-start = (bf16[512,2048]{1,0:T(8,128)(2,1)S(1)}, bf16[512,2048]{1,0:T(8,128)(2,1)}, u32[]{:S(2)}) copy-start(bf16[512,2048]{1,0:T(8,128)(2,1)} %param.18) | copy-start | bytes 6291460
  7.2 163.0 %all-gather.5.cloned.1.call-start = ((), (), s32[]{:S(2)}) async-start(), calls=%async_computation.2 | async-start | bytes 4456448 | tf_op jit(solution)/shard_map/all_gather | solution.py:14
  47.9 65.7 %copy-start.5 = (s32[2]{0:T(128)S(1)}, s32[2]{0:T(128)}, u32[]{:S(2)}) copy-start(s32[2]{0:T(128)} %param.25) | copy-start | bytes 28
  113.7 4.0 %copy-start.2 = (bf16[2,4,2048,128]{3,2,1,0:T(8,128)(2,1)S(1)}, bf16[2,4,2048,128]{3,2,1,0:T(8,128)(2,1)}, u32[]{:S(2)}) copy-start(bf16[2,4,2048,128]{3,2,1,0:T(8,128)(2,1)} %param.22) | copy-start | bytes 12582916
  117.7 1.3 copy-start.1
  117.7 1.7 copy-start.6
  117.7 1.8 copy-start.4
  117.7 2.1 copy-start.3
  121.2 128.9 %reduce-scatter.2.cloned.1.call-start = ((), (), s32[]{:S(2)}) async-start(), calls=%async_computation.1 | async-start | bytes 278528 | tf_op jit(solution)/shard_map/reduce_scatter | solution.py:163
Sparse Core Ops, SparseCore 0:
  121.3 48.8 all-gather.4
  196.0 54.0 reduce-scatter.1
where the time goes:
time: 259 us; the launch traced here: 258 us
  blocking collectives  133 us (51%)
  waiting for transfers between devices  61.5 us (24%)
  other arithmetic  27.2 us (11%)
  matrix products  18 us (7%)
  between operations  14.3 us (6%)
  local copies, waits for them, and re-layouts  3.59 us (1%)
    psum x1, blocking collectives, per_device(): whole_query, whole_fresh = lax.psum((part_query, part_fresh), 'seq')  60.7 us
    reduce_scatter x1, waiting for transfers between devices, per_device(): lax.psum_scatter(lax.dot_general(out_weight, own_attention, (((0,), (1,))...  53.5 us
    all_gather x2, blocking collectives, joined(): gathered = jax.tree.map(lambda a: lax.all_gather(a, axis), part)  37.6 us
    psum x1, blocking collectives, per_device(): squares = lax.psum(jnp.sum(hidden32 * hidden32, axis=-1), 'seq')  34.9 us
    add x15, other arithmetic, join_parts(): first_part[2] * left_factor[..., None]  18.2 us
    all_gather x1, waiting for transfers between devices, joined(): gathered = jax.tree.map(lambda a: lax.all_gather(a, axis), part)  7.9 us
    dot_general x1, matrix products, per_device(): lax.dot_general(out_weight, own_attention, (((0,), (1,)), ((), ())), pref...  5.28 us
  transfers between devices with their start and end apart: 2, of which 2 were waited for; matrix products, arithmetic and copies ran while one was open for 2% of the time, Pallas kernels for 0%

commit v1 on v0

--- a/solution.py
+++ b/solution.py
@@ -1,9 +1,14 @@
+import math
+
 import jax
 import jax.numpy as jnp
 from jax import lax
+from jax.experimental import pallas as pl
+from jax.experimental.pallas import tpu as pltpu
 from jax.sharding import PartitionSpec as P
 
 SINK_CAP = 128
+MESH = pl.DeviceIdType.MESH
 
 
 epsilon = 1e-05
@@ -172,6 +177,426 @@
     return (layer_output, new_entries.reshape(requests, drafts, 2 * kv_heads * head_dim))
 
 
+def step_kernel(
+    kind_ref, clen_ref, slen_ref, wlen_ref, hidden_ref, gain_ref,
+    qw_hbm, kvw_hbm, ow_hbm, rk_hbm, rv_hbm, sk_hbm, sv_hbm,
+    out_ref, new_ref,
+    w_buf, o_buf, rk, rv, sk, sv,
+    sq_send, sq_recv, sib_send, sib_recv, rs_send, rs_recv, ag,
+    a_res, stat_cols, a_send, a_recv, st_send, st_recv, o_send, o_recv,
+    load_sem, cache_sem, send_sem, recv_sem,
+):
+    f32, bf16 = jnp.float32, jnp.bfloat16
+    n = lax.axis_size("seq")
+    me = lax.axis_index("seq")
+    core, chip, chips = lax.rem(me, 2), me // 2, n // 2
+    sibling = me + 1 - 2 * core
+    requests, drafts, width = hidden_ref.shape
+    tokens = requests * drafts
+    kv_heads = kind_ref.shape[0]
+    retrieval, running = rk.shape[1], sk.shape[1]
+    head_dim = rk.shape[3]
+    own_width = o_buf.shape[1]
+    heads = own_width // head_dim
+    share = n // kv_heads
+    half_rows = heads * drafts
+    own_rows = requests * half_rows
+    group_rows = share * half_rows
+    score_scale = head_dim ** (-0.5)
+    exp_scale = score_scale * math.log2(math.e)
+    SQ, SIB, RS, AG, ATT, STAT, OUT = range(7)
+
+    def remote(kind, src, dst, send_slot, recv_slot, target):
+        return pltpu.make_async_remote_copy(
+            src_ref=src, dst_ref=dst,
+            send_sem=send_sem.at[kind, send_slot], recv_sem=recv_sem.at[kind, recv_slot],
+            device_id={"seq": target}, device_id_type=MESH,
+        )
+
+    def peer(step):
+        return lax.rem(me + step, n)
+
+    def each_peer(body):
+        def run(step, carry):
+            body(step, peer(step))
+            return carry
+        lax.fori_loop(1, n, run, 0)
+
+    def chunk_owner(i):
+        other = i < chips
+        j = lax.rem(i, chips)
+        target_chip = lax.rem(chip + 1 + j, chips)
+        return 2 * target_chip + jnp.where(other, 1 - core, core)
+
+    def weight_copies(i):
+        p = chunk_owner(i)
+        qcols = pl.ds(pl.multiple_of(p * own_width, own_width), own_width)
+        kcols = pl.ds(pl.multiple_of(p * head_dim, head_dim), head_dim)
+        return (
+            pltpu.make_async_copy(qw_hbm.at[:, qcols], w_buf.at[i, :, pl.ds(0, own_width)], load_sem.at[0, i]),
+            pltpu.make_async_copy(kvw_hbm.at[:, kcols], w_buf.at[i, :, pl.ds(own_width, head_dim)], load_sem.at[1, i]),
+        )
+
+    def out_copy(i):
+        p = lax.rem(me + 1 + i, n)
+        cols = pl.ds(pl.multiple_of(p * width, width), width)
+        return pltpu.make_async_copy(ow_hbm.at[:, cols], o_buf.at[i], load_sem.at[2, i])
+
+    def start_weights(i, carry):
+        for copy in weight_copies(i):
+            copy.start()
+        return carry
+
+    lax.fori_loop(0, n, start_weights, 0)
+
+    barrier = pltpu.get_barrier_semaphore()
+    each_peer(lambda step, target: pl.semaphore_signal(
+        barrier, inc=1, device_id={"seq": target}, device_id_type=MESH))
+
+    hidden32 = jnp.concatenate([hidden_ref[b].astype(f32) for b in range(requests)], axis=0)
+    squares = jnp.sum(hidden32 * hidden32, axis=-1, keepdims=True)
+    eye = (lax.broadcasted_iota(jnp.int32, (tokens, 128), 0)
+           == lax.broadcasted_iota(jnp.int32, (tokens, 128), 1))
+    sq_send[...] = jnp.sum(jnp.where(eye, squares, 0.0), axis=0, keepdims=True)
+    sq_recv[me] = sq_send[...]
+    stat_cols[...] = jnp.zeros_like(stat_cols)
+    pl.semaphore_wait(barrier, n - 1)
+
+    def sq_copy(step, target, source):
+        return remote(SQ, sq_send, sq_recv.at[source], step, source, target)
+
+    each_peer(lambda step, target: sq_copy(step, target, me).start())
+
+    cache_copies = [
+        (pltpu.make_async_copy(sk_hbm, sk, cache_sem.at[0, 0]),
+         pltpu.make_async_copy(sv_hbm, sv, cache_sem.at[1, 0])),
+    ]
+    for b in range(requests):
+        cache_copies.append(
+            (pltpu.make_async_copy(rk_hbm.at[b], rk.at[b], cache_sem.at[0, 1 + b]),
+             pltpu.make_async_copy(rv_hbm.at[b], rv.at[b], cache_sem.at[1, 1 + b])))
+    for pair in cache_copies:
+        for copy in pair:
+            copy.start()
+
+    each_peer(lambda step, source: sq_copy(step, source, source).wait_recv())
+    total_row = sq_recv[0]
+    for s in range(1, n):
+        total_row = total_row + sq_recv[s]
+    total_sq = jnp.sum(jnp.where(eye, total_row, 0.0), axis=1, keepdims=True)
+    inverse = lax.rsqrt(total_sq / (width * n) + epsilon)
+    normed = (hidden32 * inverse * gain_ref[...].astype(f32)).astype(bf16)
+
+    def project(i):
+        for copy in weight_copies(i):
+            copy.wait()
+        return jnp.dot(normed, w_buf[i], preferred_element_type=f32)
+
+    def sib_copy(j):
+        return remote(SIB, sib_send.at[j], sib_recv.at[j], j, j, sibling)
+
+    def first_half(j, carry):
+        sib_send[j] = project(j)
+        sib_copy(j).start()
+        return carry
+
+    lax.fori_loop(0, chips, first_half, 0)
+
+    def rs_copy(j):
+        target = 2 * lax.rem(chip + 1 + j, chips) + core
+        return remote(RS, rs_send.at[j], rs_recv.at[j], j, j, target)
+
+    def second_half(j, carry):
+        value = project(chips + j)
+        sib_copy(j).wait_recv()
+        rs_send[j] = value + sib_recv[j]
+        rs_copy(j).start()
+        return carry
+
+    lax.fori_loop(0, chips - 1, second_half, 0)
+    own = project(n - 1)
+    sib_copy(chips - 1).wait_recv()
+    own = own + sib_recv[chips - 1]
+
+    def start_out(i, carry):
+        out_copy(i).start()
+        return carry
+
+    lax.fori_loop(0, n, start_out, 0)
+
+    for j in range(chips - 1):
+        rs_copy(j).wait_recv()
+        own = own + rs_recv[j]
+
+    def by_head(values):
+        return jnp.concatenate(
+            [values[b * drafts:(b + 1) * drafts, h * head_dim:(h + 1) * head_dim]
+             for b in range(requests) for h in range(heads)], axis=0)
+
+    packed = jnp.concatenate(
+        [by_head(own[:, :own_width]), own[:, own_width:],
+         jnp.zeros((ag.shape[1] - own_rows - tokens, head_dim), f32)], axis=0)
+    ag[me] = packed.astype(bf16)
+
+    def ag_copy(step, target, source):
+        return remote(AG, ag.at[source], ag.at[source], step, source, target)
+
+    each_peer(lambda step, target: ag_copy(step, target, me).start())
+
+    kinds = [kind_ref[g] for g in range(kv_heads)]
+    slot_of, before = [], 0
+    for g in range(kv_heads):
+        slot = jnp.where(kinds[g] == 1, before, retrieval + g - before)
+        slot_of.append(jnp.minimum(slot, retrieval + running - 1))
+        before = before + kinds[g]
+    head_of = []
+    for j in range(retrieval + running):
+        found = 0
+        for g in range(kv_heads):
+            found = found + jnp.where(slot_of[g] == j, g, 0)
+        head_of.append(jnp.minimum(found, kv_heads - 1))
+
+    each_peer(lambda step, source: ag_copy(step, source, source).wait_recv())
+
+    for p in range(n):
+        piece = ag[p, own_rows:, :]
+        for b in range(requests):
+            new_ref[b, :, p * head_dim:(p + 1) * head_dim] = piece[b * drafts:(b + 1) * drafts]
+
+    def attend(b, j, keys, values, visible):
+        q = ag[pl.ds(share * head_of[j], share), b * half_rows:(b + 1) * half_rows, :]
+        q = q.reshape(group_rows, head_dim)
+        scores = lax.dot_general(q, keys, (((1,), (1,)), ((), ())), preferred_element_type=f32)
+        scores = jnp.where(visible, scores, floor_score)
+        peak = jnp.max(scores, axis=-1, keepdims=True)
+        weights = jnp.exp2((scores - peak) * exp_scale)
+        total = jnp.sum(weights, axis=-1, keepdims=True)
+        block = jnp.dot(weights.astype(bf16), values, preferred_element_type=f32)
+        a_res[j, :, b * half_rows:(b + 1) * half_rows, :] = block.astype(bf16).reshape(
+            share, half_rows, head_dim)
+        lane = lax.broadcasted_iota(jnp.int32, (half_rows, 128), 1)
+        for at, column in ((0, peak * score_scale), (own_rows, total)):
+            rows = pl.ds(at + b * half_rows, half_rows)
+            kept = stat_cols[rows, :]
+            for s in range(share):
+                kept = jnp.where(lane == share * head_of[j] + s,
+                                 column[s * half_rows:(s + 1) * half_rows], kept)
+            stat_cols[rows, :] = kept
+
+    for copy in cache_copies[0]:
+        copy.wait()
+    slots = sk.shape[2]
+    slot_pos = me * slots + lax.broadcasted_iota(jnp.int32, (1, slots), 1)
+    positions = rk.shape[2]
+    cache_pos = me * positions + lax.broadcasted_iota(jnp.int32, (1, positions), 1)
+    for b in range(requests):
+        seen = (slot_pos < slen_ref[b]) | (
+            (slot_pos >= SINK_CAP) & (slot_pos < SINK_CAP + wlen_ref[b]))
+        for r in range(running):
+            attend(b, retrieval + r, sk[b, r], sv[b, r], seen)
+    for b in range(requests):
+        for copy in cache_copies[1 + b]:
+            copy.wait()
+        seen = cache_pos < clen_ref[b]
+        for r in range(retrieval):
+            attend(b, r, rk[b, r], rv[b, r], seen)
+
+    stat_rows = stat_cols[...].T
+    for p in range(n):
+        st_send[p] = stat_rows[p:p + 1, :]
+    for g in range(kv_heads):
+        a_send[g * share:(g + 1) * share] = a_res[slot_of[g]]
+    st_recv[me] = st_send[me]
+    a_recv[me] = a_send[me]
+
+    def att_copy(step, target, source):
+        return remote(ATT, a_send.at[target], a_recv.at[source], step, source, target)
+
+    def st_copy(step, target, source):
+        return remote(STAT, st_send.at[target], st_recv.at[source], step, source, target)
+
+    def send_attention(step, target):
+        st_copy(step, target, me).start()
+        att_copy(step, target, me).start()
+
+    each_peer(send_attention)
+
+    own_head = me // share
+    own_q = ag[me, 0:own_rows, :]
+    new_keys = ag[own_head, own_rows:, :]
+    new_values = ag[kv_heads + own_head, own_rows:, :]
+    new_rows = ag.shape[1] - own_rows
+    scores = lax.dot_general(own_q, new_keys, (((1,), (1,)), ((), ())), preferred_element_type=f32)
+    scores = scores * score_scale
+    row = lax.broadcasted_iota(jnp.int32, (own_rows, new_rows), 0)
+    col = lax.broadcasted_iota(jnp.int32, (own_rows, new_rows), 1)
+    row_bits, col_bits = half_rows.bit_length() - 1, drafts.bit_length() - 1
+    same = lax.shift_right_logical(row, row_bits) == lax.shift_right_logical(col, col_bits)
+    visible = same & ((col & (drafts - 1)) <= (row & (drafts - 1)))
+    scores = jnp.where(visible, scores, floor_score)
+    new_peak = jnp.max(scores, axis=-1, keepdims=True)
+    new_weights = jnp.where(visible, jnp.exp(scores - new_peak), 0.0)
+    new_total = jnp.sum(new_weights, axis=-1, keepdims=True)
+    new_out = jnp.dot(new_weights.astype(bf16), new_values, preferred_element_type=f32)
+
+    def wait_attention(step, source):
+        st_copy(step, source, source).wait_recv()
+        att_copy(step, source, source).wait_recv()
+
+    each_peer(wait_attention)
+    stats = jnp.concatenate(
+        [st_recv[s] for s in range(n)] + [jnp.zeros((128 - n, 128), f32)], axis=0).T
+    lane = lax.broadcasted_iota(jnp.int32, (own_rows, 128), 1)
+    peaks = jnp.where(lane < n, stats[0:own_rows], floor_score)
+    totals = stats[own_rows:2 * own_rows]
+    top = jnp.maximum(jnp.max(peaks, axis=-1, keepdims=True), new_peak)
+    factors = jnp.exp(peaks - top)
+    new_factor = jnp.exp(new_peak - top)
+    denominator = jnp.sum(factors * totals, axis=-1, keepdims=True) + new_factor * new_total
+    numerator = new_factor * new_out
+    for s in range(n):
+        numerator = numerator + factors[:, s:s + 1] * a_recv[s].astype(f32)
+    attended = numerator / denominator
+    attention = jnp.concatenate(
+        [jnp.concatenate(
+            [attended[b * half_rows + h * drafts:b * half_rows + (h + 1) * drafts]
+             for b in range(requests)], axis=0) for h in range(heads)], axis=1).astype(bf16)
+
+    half_width = width // 2
+
+    def out_part(i):
+        out_copy(i).wait()
+        part = jnp.dot(attention, o_buf[i], preferred_element_type=f32)
+        return jnp.concatenate([part[:, :half_width], part[:, half_width:]], axis=0)
+
+    def o_copy(step, target, source):
+        return remote(OUT, o_send.at[step], o_recv.at[source], step, source, target)
+
+    def send_out(step, target):
+        o_send[step] = out_part(step - 1).astype(bf16)
+        o_copy(step, target, me).start()
+
+    each_peer(send_out)
+    result = out_part(n - 1)
+
+    def take_out(step, total):
+        source = peer(step)
+        o_copy(step, source, source).wait_recv()
+        return total + o_recv[source].astype(f32)
+
+    result = lax.fori_loop(1, n, take_out, result)
+    result = jnp.concatenate([result[:tokens], result[tokens:]], axis=1).astype(bf16)
+    for b in range(requests):
+        out_ref[b] = result[b * drafts:(b + 1) * drafts]
+
+    def finish(step, target):
+        sq_copy(step, target, me).wait_send()
+        ag_copy(step, target, me).wait_send()
+        st_copy(step, target, me).wait_send()
+        att_copy(step, target, me).wait_send()
+        o_copy(step, target, me).wait_send()
+
+    each_peer(finish)
+    for j in range(chips):
+        sib_copy(j).wait_send()
+    for j in range(chips - 1):
+        rs_copy(j).wait_send()
+
+
+def fused_device(
+    hidden, norm_gain, q_weight, kv_weight, out_weight, head_kind,
+    ret_keys, ret_values, stream_keys, stream_values, cache_len, sink_len, window_len,
+):
+    n = lax.axis_size("seq")
+    requests, drafts, width = hidden.shape
+    tokens = requests * drafts
+    head_dim = ret_keys.shape[3]
+    own_width = out_weight.shape[0]
+    own_rows = tokens * (own_width // head_dim)
+    slots = ret_keys.shape[1] + stream_keys.shape[1]
+    share = n // slots
+    chips = n // 2
+    piece = own_width + head_dim
+    f32, bf16 = jnp.float32, jnp.bfloat16
+    smem = pl.BlockSpec(memory_space=pltpu.SMEM)
+    vmem = pl.BlockSpec(memory_space=pltpu.VMEM)
+    hbm = pl.BlockSpec(memory_space=pltpu.HBM)
+    scratch = [
+        pltpu.VMEM((n, width, piece), bf16),
+        pltpu.VMEM((n, own_width, width), bf16),
+        pltpu.VMEM(ret_keys.shape, bf16),
+        pltpu.VMEM(ret_values.shape, bf16),
+        pltpu.VMEM(stream_keys.shape, bf16),
+        pltpu.VMEM(stream_values.shape, bf16),
+        pltpu.VMEM((1, 128), f32),
+        pltpu.VMEM((n, 1, 128), f32),
+        pltpu.VMEM((chips, tokens, piece), f32),
+        pltpu.VMEM((chips, tokens, piece), f32),
+        pltpu.VMEM((chips, tokens, piece), f32),
+        pltpu.VMEM((chips, tokens, piece), f32),
+        pltpu.VMEM((n, own_rows + 16, head_dim), bf16),
+        pltpu.VMEM((slots, share, own_rows, head_dim), bf16),
+        pltpu.VMEM((128, 128), f32),
+        pltpu.VMEM((n, own_rows, head_dim), bf16),
+        pltpu.VMEM((n, own_rows, head_dim), bf16),
+        pltpu.VMEM((n, 1, 128), f32),
+        pltpu.VMEM((n, 1, 128), f32),
+        pltpu.VMEM((n, 2 * tokens, width // 2), bf16),
+        pltpu.VMEM((n, 2 * tokens, width // 2), bf16),
+        pltpu.SemaphoreType.DMA((3, n)),
+        pltpu.SemaphoreType.DMA((2, 1 + requests)),
+        pltpu.SemaphoreType.DMA((7, n)),
+        pltpu.SemaphoreType.DMA((7, n)),
+    ]
+    return pl.pallas_call(
+        step_kernel,
+        out_shape=(
+            jax.ShapeDtypeStruct(hidden.shape, bf16),
+            jax.ShapeDtypeStruct((requests, drafts, kv_weight.shape[1]), bf16),
+        ),
+        in_specs=[smem] * 4 + [vmem] * 2 + [hbm] * 7,
+        out_specs=(vmem, vmem),
+        scratch_shapes=scratch,
+        compiler_params=pltpu.CompilerParams(
+            collective_id=0, has_side_effects=True, vmem_limit_bytes=52 * 2**20
+        ),
+        name="decode_step",
+    )(
+        head_kind, cache_len, sink_len, window_len, hidden, norm_gain.reshape(1, width),
+        q_weight, kv_weight, out_weight, ret_keys, ret_values, stream_keys, stream_values,
+    )
+
+
+def power_of_two(value):
+    return value & (value - 1) == 0
+
+
+def fused_fits(
+    hidden, norm_gain, q_weight, kv_weight, out_weight, head_kind,
+    ret_keys, ret_values, stream_keys, stream_values, cache_len, sink_len, window_len,
+):
+    n = lax.axis_size("seq")
+    requests, drafts, width = hidden.shape
+    tokens = requests * drafts
+    head_dim = ret_keys.shape[3]
+    own_width = out_weight.shape[0]
+    kv_heads = head_kind.shape[0]
+    heads = own_width // head_dim
+    return (
+        n % 2 == 0 and n <= 128 and n % kv_heads == 0 and tokens == 8
+        and head_dim == 128 and width % 256 == 0 and own_width % head_dim == 0
+        and q_weight.shape[1] == n * own_width and kv_weight.shape[1] == n * head_dim
+        and n == 2 * kv_heads and power_of_two(heads * drafts) and power_of_two(drafts)
+        and heads * drafts % 16 == 0 and 2 * tokens * heads <= 128
+        and ret_keys.shape[2] % 128 == 0 and stream_keys.shape[2] % 128 == 0
+        and ret_keys.shape[1] + stream_keys.shape[1] == kv_heads
+    )
+
+
+def step_device(*args):
+    return fused_device(*args) if fused_fits(*args) else per_device(*args)
+
+
 def solution(mesh):
     in_specs = (
         P("groups", None, "seq"),
@@ -190,5 +615,5 @@
     )
     out_specs = (P("groups", None, "seq"), P("groups", None, None))
     return jax.shard_map(
-        per_device, mesh=mesh, in_specs=in_specs, out_specs=out_specs, check_vma=False
-    )
+        step_device, mesh=mesh, in_specs=in_specs, out_specs=out_specs, check_vma=False
+    )

time: 259 us -> 50.7 us (0.20)
  blocking collectives: 133 us -> 0 us
  waiting for transfers between devices: 61.5 us -> 0 us
  Pallas kernels: 0 us -> 42.6 us
  other arithmetic: 27.2 us -> 0 us
  matrix products: 18 us -> 0 us
  between operations: 14.3 us -> 0.65 us
  local copies, waits for them, and re-layouts: 3.59 us -> 7.11 us
    psum x2 -> x0, blocking collectives: 95.5 us -> none  [the longest x1 60.7 us: per_device(): whole_query, whole_fresh = lax.psum((part_query, part_fresh), 'seq')]
    reduce_scatter x1 -> x0, waiting for transfers between devices: 53.5 us -> none  [per_device(): lax.psum_scatter(lax.dot_general(out_weight, own_attention, (((0,), (1,))...]
    pallas_call x0 -> x1, Pallas kernels: none -> 42.6 us  [fused_device(): pl.pallas_call(step_kernel, out_shape=(jax.ShapeDtypeStruct(hidden.shape,...]
    all_gather x2 -> x0, blocking collectives: 37.6 us -> none  [joined(): gathered = jax.tree.map(lambda a: lax.all_gather(a, axis), part)]
    add x34 -> x0, other arithmetic: 19.2 us -> none  [the longest x15 18.2 us: join_parts(): first_part[2] * left_factor[..., None]]
    dot_general x17 -> x0, matrix products: 18 us -> none  [the longest x1 5.28 us: per_device(): lax.dot_general(out_weight, own_attention, (((0,), (1,)), ((), ())), pref...]
    all_gather x1 -> x0, waiting for transfers between devices: 7.9 us -> none  [joined(): gathered = jax.tree.map(lambda a: lax.all_gather(a, axis), part)]
    unnamed x16, local copies, waits for them, and re-layouts: 0.49 us -> 6.43 us
  transfers between devices with their start and end apart: 2 -> 0, of which waited for: 2 -> 0; matrix products, arithmetic and copies ran while one was open for 2% -> 0% of each run, Pallas kernels for 0% -> 0%
where the time goes in v1:
time: 50.7 us; the launch traced here: 50.4 us
  Pallas kernels  42.6 us (84%)
  local copies, waits for them, and re-layouts  7.11 us (14%)
  between operations  0.65 us (1%)
    pallas_call x1, Pallas kernels, fused_device(): pl.pallas_call(step_kernel, out_shape=(jax.ShapeDtypeStruct(hidden.shape,...  42.6 us
    unnamed x16, local copies, waits for them, and re-layouts  6.43 us

profile of v1, /device:TPU:0, one launch (start us, length us, event | category | flops | bytes accessed | tf_op | source)
XLA Modules:
  0.0 50.4 jit_solution(9099009954004061747)
XLA Ops:
  0.6 0.7 %reshape.7.gain_ref = bf16[1,512]{1,0:T(2,128)(2,1)S(1)} reshape(bf16[512]{0:T(512)(128)(2,1)} %param.14) | data formatting | bytes 2048 | tf_op jit(solution)/shard_map/reshape | solution.py:565
  1.3 0.0 copy-start
  1.3 0.9 %copy-done = bf16[2,4,128,128]{3,2,1,0:T(8,128)(2,1)S(1)} copy-done((bf16[2,4,128,128]{3,2,1,0:T(8,128)(2,1)S(1)}, bf16[2,4,128,128]{3,2,1,0:T(8,128)(2,1)}, u32[]{:S(2)}) %copy-start) | copy-done | bytes 262168
  2.3 0.0 copy-start.1
  2.3 0.9 %copy-done.1 = bf16[2,4,128,128]{3,2,1,0:T(8,128)(2,1)S(1)} copy-done((bf16[2,4,128,128]{3,2,1,0:T(8,128)(2,1)S(1)}, bf16[2,4,128,128]{3,2,1,0:T(8,128)(2,1)}, u32[]{:S(2)}) %copy-start.1) | copy-done | bytes 262168
  3.2 0.0 copy-start.2
  3.2 0.7 %copy-done.2 = bf16[2,4,512]{2,1,0:T(4,128)(2,1)S(1)} copy-done((bf16[2,4,512]{2,1,0:T(4,128)(2,1)S(1)}, bf16[2,4,512]{2,1,0:T(4,128)(2,1)}, u32[]{:S(2)}) %copy-start.2) | copy-done | bytes 8216
  3.9 0.0 copy-start.3
  3.9 0.7 %copy-done.3 = s32[8]{0:T(128)S(1)} copy-done((s32[8]{0:T(128)S(1)}, s32[8]{0:T(128)}, u32[]{:S(2)}) %copy-start.3) | copy-done | bytes 56
  4.6 0.0 copy-start.4
  4.6 0.7 %copy-done.4 = s32[2]{0:T(128)S(1)} copy-done((s32[2]{0:T(128)S(1)}, s32[2]{0:T(128)}, u32[]{:S(2)}) %copy-start.4) | copy-done | bytes 32
  5.2 0.0 copy-start.5
  5.2 0.7 %copy-done.5 = s32[2]{0:T(128)S(1)} copy-done((s32[2]{0:T(128)S(1)}, s32[2]{0:T(128)}, u32[]{:S(2)}) %copy-start.5) | copy-done | bytes 32
  5.9 0.0 copy-start.6
  5.9 0.7 %copy-done.6 = s32[2]{0:T(128)S(1)} copy-done((s32[2]{0:T(128)S(1)}, s32[2]{0:T(128)}, u32[]{:S(2)}) %copy-start.6) | copy-done | bytes 32
  6.5 42.6 %decode_step.1 = (bf16[2,4,512]{2,1,0:T(4,128)(2,1)S(1)}, bf16[2,4,2048]{2,1,0:T(4,128)(2,1)S(1)}) custom-call(s32[8]{0:T(128)S(1)} %copy-done.3, s32[2]{0:T(128)S(1)} %copy-done.4, s32[2]{0:T(128)S(1)} %copy-done.5, s32[2]{0:T(128)S(1)} %copy-done.6, bf16[2,4,512]{2,1,0:T(4,128)(2,1)S(1)} %copy-done.2, bf16[1,512]{1,0:T(2,128)(2,1)S(1)} %reshape.7.gain_ref, ...), custom_call_target="tpu_custom_call" | custom-call | tf_op jit(solution)/shard_map/decode_step/pallas_call | solution.py:551
  49.2 0.6 %copy.17 = bf16[2,4,512]{2,1,0:T(4,128)(2,1)} copy(bf16[2,4,512]{2,1,0:T(4,128)(2,1)S(1)} %get-tuple-element.4) | data formatting | bytes 16384
  49.8 0.6 %copy.18 = bf16[2,4,2048]{2,1,0:T(4,128)(2,1)} copy(bf16[2,4,2048]{2,1,0:T(4,128)(2,1)S(1)} %get-tuple-element.5) | data formatting | bytes 65536
Async XLA Ops:
  1.3 0.9 %copy-start = (bf16[2,4,128,128]{3,2,1,0:T(8,128)(2,1)S(1)}, bf16[2,4,128,128]{3,2,1,0:T(8,128)(2,1)}, u32[]{:S(2)}) copy-start(bf16[2,4,128,128]{3,2,1,0:T(8,128)(2,1)} %sk_hbm.1) | copy-start | bytes 786436
  2.3 0.9 %copy-start.1 = (bf16[2,4,128,128]{3,2,1,0:T(8,128)(2,1)S(1)}, bf16[2,4,128,128]{3,2,1,0:T(8,128)(2,1)}, u32[]{:S(2)}) copy-start(bf16[2,4,128,128]{3,2,1,0:T(8,128)(2,1)} %sv_hbm.1) | copy-start | bytes 786436
  3.2 0.7 %copy-start.2 = (bf16[2,4,512]{2,1,0:T(4,128)(2,1)S(1)}, bf16[2,4,512]{2,1,0:T(4,128)(2,1)}, u32[]{:S(2)}) copy-start(bf16[2,4,512]{2,1,0:T(4,128)(2,1)} %hidden_ref.1) | copy-start | bytes 24580
  3.9 0.7 %copy-start.3 = (s32[8]{0:T(128)S(1)}, s32[8]{0:T(128)}, u32[]{:S(2)}) copy-start(s32[8]{0:T(128)} %kind_ref.1) | copy-start | bytes 100
  4.6 0.7 %copy-start.4 = (s32[2]{0:T(128)S(1)}, s32[2]{0:T(128)}, u32[]{:S(2)}) copy-start(s32[2]{0:T(128)} %clen_ref.1) | copy-start | bytes 28
  5.2 0.7 %copy-start.5 = (s32[2]{0:T(128)S(1)}, s32[2]{0:T(128)}, u32[]{:S(2)}) copy-start(s32[2]{0:T(128)} %slen_ref.1) | copy-start | bytes 28
  5.9 0.7 %copy-start.6 = (s32[2]{0:T(128)S(1)}, s32[2]{0:T(128)}, u32[]{:S(2)}) copy-start(s32[2]{0:T(128)} %wlen_ref.1) | copy-start | bytes 28

commit v2 on v1

--- a/solution.py
+++ b/solution.py
@@ -9,6 +9,7 @@
 
 SINK_CAP = 128
 MESH = pl.DeviceIdType.MESH
+GROUP = 4
 
 
 epsilon = 1e-05
@@ -178,13 +179,14 @@
 
 
 def step_kernel(
-    kind_ref, clen_ref, slen_ref, wlen_ref, hidden_ref, gain_ref,
+    kind_hbm, clen_hbm, slen_hbm, wlen_hbm, hidden_hbm, gain_hbm,
     qw_hbm, kvw_hbm, ow_hbm, rk_hbm, rv_hbm, sk_hbm, sv_hbm,
     out_ref, new_ref,
+    kind_ref, clen_ref, slen_ref, wlen_ref, hidden_ref, gain_ref,
     w_buf, o_buf, rk, rv, sk, sv,
     sq_send, sq_recv, sib_send, sib_recv, rs_send, rs_recv, ag,
     a_res, stat_cols, a_send, a_recv, st_send, st_recv, o_send, o_recv,
-    load_sem, cache_sem, send_sem, recv_sem,
+    small_sem, load_sem, cache_sem, send_sem, recv_sem,
 ):
     f32, bf16 = jnp.float32, jnp.bfloat16
     n = lax.axis_size("seq")
@@ -197,6 +199,7 @@
     retrieval, running = rk.shape[1], sk.shape[1]
     head_dim = rk.shape[3]
     own_width = o_buf.shape[1]
+    piece = own_width + head_dim
     heads = own_width // head_dim
     share = n // kv_heads
     half_rows = heads * drafts
@@ -223,36 +226,47 @@
         lax.fori_loop(1, n, run, 0)
 
     def chunk_owner(i):
-        other = i < chips
-        j = lax.rem(i, chips)
-        target_chip = lax.rem(chip + 1 + j, chips)
-        return 2 * target_chip + jnp.where(other, 1 - core, core)
+        target_chip = lax.rem(chip + 1 + i % chips, chips)
+        return 2 * target_chip + (1 - core if i < chips else core)
 
     def weight_copies(i):
         p = chunk_owner(i)
         qcols = pl.ds(pl.multiple_of(p * own_width, own_width), own_width)
         kcols = pl.ds(pl.multiple_of(p * head_dim, head_dim), head_dim)
+        at = (i % GROUP) * piece
         return (
-            pltpu.make_async_copy(qw_hbm.at[:, qcols], w_buf.at[i, :, pl.ds(0, own_width)], load_sem.at[0, i]),
-            pltpu.make_async_copy(kvw_hbm.at[:, kcols], w_buf.at[i, :, pl.ds(own_width, head_dim)], load_sem.at[1, i]),
+            pltpu.make_async_copy(
+                qw_hbm.at[:, qcols], w_buf.at[i // GROUP, :, pl.ds(at, own_width)],
+                load_sem.at[0, i]),
+            pltpu.make_async_copy(
+                kvw_hbm.at[:, kcols], w_buf.at[i // GROUP, :, pl.ds(at + own_width, head_dim)],
+                load_sem.at[1, i]),
         )
 
     def out_copy(i):
         p = lax.rem(me + 1 + i, n)
         cols = pl.ds(pl.multiple_of(p * width, width), width)
-        return pltpu.make_async_copy(ow_hbm.at[:, cols], o_buf.at[i], load_sem.at[2, i])
-
-    def start_weights(i, carry):
+        return pltpu.make_async_copy(
+            ow_hbm.at[:, cols], o_buf.at[i // GROUP, :, pl.ds((i % GROUP) * width, width)],
+            load_sem.at[2, i])
+
+    small = [
+        pltpu.make_async_copy(src, dst, small_sem.at[at]) for at, (src, dst) in enumerate((
+            (hidden_hbm, hidden_ref), (gain_hbm, gain_ref), (kind_hbm, kind_ref),
+            (clen_hbm, clen_ref), (slen_hbm, slen_ref), (wlen_hbm, wlen_ref)))
+    ]
+    for copy in small:
+        copy.start()
+    for i in range(n):
         for copy in weight_copies(i):
             copy.start()
-        return carry
-
-    lax.fori_loop(0, n, start_weights, 0)
 
     barrier = pltpu.get_barrier_semaphore()
     each_peer(lambda step, target: pl.semaphore_signal(
         barrier, inc=1, device_id={"seq": target}, device_id_type=MESH))
 
+    for copy in small:
+        copy.wait()
     hidden32 = jnp.concatenate([hidden_ref[b].astype(f32) for b in range(requests)], axis=0)
     squares = jnp.sum(hidden32 * hidden32, axis=-1, keepdims=True)
     eye = (lax.broadcasted_iota(jnp.int32, (tokens, 128), 0)
@@ -285,44 +299,40 @@
         total_row = total_row + sq_recv[s]
     total_sq = jnp.sum(jnp.where(eye, total_row, 0.0), axis=1, keepdims=True)
     inverse = lax.rsqrt(total_sq / (width * n) + epsilon)
-    normed = (hidden32 * inverse * gain_ref[...].astype(f32)).astype(bf16)
-
-    def project(i):
-        for copy in weight_copies(i):
-            copy.wait()
-        return jnp.dot(normed, w_buf[i], preferred_element_type=f32)
+    normed = (hidden32 * inverse * gain_ref[...].astype(f32).reshape(1, width)).astype(bf16)
+
+    def project(group):
+        for i in range(group * GROUP, (group + 1) * GROUP):
+            for copy in weight_copies(i):
+                copy.wait()
+        whole = jnp.dot(normed, w_buf[group], preferred_element_type=f32)
+        return [whole[:, at * piece:(at + 1) * piece] for at in range(GROUP)]
 
     def sib_copy(j):
         return remote(SIB, sib_send.at[j], sib_recv.at[j], j, j, sibling)
 
-    def first_half(j, carry):
-        sib_send[j] = project(j)
-        sib_copy(j).start()
-        return carry
-
-    lax.fori_loop(0, chips, first_half, 0)
+    for group in range(chips // GROUP):
+        for at, value in enumerate(project(group)):
+            sib_send[group * GROUP + at] = value
+        for at in range(GROUP):
+            sib_copy(group * GROUP + at).start()
 
     def rs_copy(j):
         target = 2 * lax.rem(chip + 1 + j, chips) + core
         return remote(RS, rs_send.at[j], rs_recv.at[j], j, j, target)
 
-    def second_half(j, carry):
-        value = project(chips + j)
-        sib_copy(j).wait_recv()
-        rs_send[j] = value + sib_recv[j]
-        rs_copy(j).start()
-        return carry
-
-    lax.fori_loop(0, chips - 1, second_half, 0)
-    own = project(n - 1)
-    sib_copy(chips - 1).wait_recv()
-    own = own + sib_recv[chips - 1]
-
-    def start_out(i, carry):
+    for group in range(chips // GROUP):
+        values = project(chips // GROUP + group)
+        for at, value in enumerate(values):
+            j = group * GROUP + at
+            sib_copy(j).wait_recv()
+            own = value + sib_recv[j]
+            if j < chips - 1:
+                rs_send[j] = own
+                rs_copy(j).start()
+
+    for i in range(n):
         out_copy(i).start()
-        return carry
-
-    lax.fori_loop(0, n, start_out, 0)
 
     for j in range(chips - 1):
         rs_copy(j).wait_recv()
@@ -335,13 +345,23 @@
 
     packed = jnp.concatenate(
         [by_head(own[:, :own_width]), own[:, own_width:],
-         jnp.zeros((ag.shape[1] - own_rows - tokens, head_dim), f32)], axis=0)
-    ag[me] = packed.astype(bf16)
+         jnp.zeros((ag.shape[2] - own_rows - tokens, head_dim), f32)], axis=0)
+    ag[core, chip] = packed.astype(bf16)
 
     def ag_copy(step, target, source):
-        return remote(AG, ag.at[source], ag.at[source], step, source, target)
-
-    each_peer(lambda step, target: ag_copy(step, target, me).start())
+        return remote(
+            AG, ag.at[core, source], ag.at[core, source], step, source, 2 * target + core)
+
+    def each_chip(body):
+        def run(step, carry):
+            body(step, lax.rem(chip + step, chips))
+            return carry
+        lax.fori_loop(1, chips, run, 0)
+
+    def pair_copy(side):
+        return remote(AG, ag.at[side], ag.at[side], chips, chips, sibling)
+
+    each_chip(lambda step, target: ag_copy(step, target, chip).start())
 
     kinds = [kind_ref[g] for g in range(kv_heads)]
     slot_of, before = [], 0
@@ -356,16 +376,19 @@
             found = found + jnp.where(slot_of[g] == j, g, 0)
         head_of.append(jnp.minimum(found, kv_heads - 1))
 
-    each_peer(lambda step, source: ag_copy(step, source, source).wait_recv())
+    each_chip(lambda step, source: ag_copy(step, source, source).wait_recv())
+    pair_copy(core).start()
+    pair_copy(1 - core).wait_recv()
 
     for p in range(n):
-        piece = ag[p, own_rows:, :]
+        entries = ag[p % 2, p // 2, own_rows:, :]
         for b in range(requests):
-            new_ref[b, :, p * head_dim:(p + 1) * head_dim] = piece[b * drafts:(b + 1) * drafts]
+            new_ref[b, :, p * head_dim:(p + 1) * head_dim] = entries[b * drafts:(b + 1) * drafts]
 
     def attend(b, j, keys, values, visible):
-        q = ag[pl.ds(share * head_of[j], share), b * half_rows:(b + 1) * half_rows, :]
-        q = q.reshape(group_rows, head_dim)
+        q = jnp.concatenate(
+            [ag[s % 2, head_of[j] * share // 2 + s // 2, b * half_rows:(b + 1) * half_rows, :]
+             for s in range(share)], axis=0)
         scores = lax.dot_general(q, keys, (((1,), (1,)), ((), ())), preferred_element_type=f32)
         scores = jnp.where(visible, scores, floor_score)
         peak = jnp.max(scores, axis=-1, keepdims=True)
@@ -422,10 +445,10 @@
     each_peer(send_attention)
 
     own_head = me // share
-    own_q = ag[me, 0:own_rows, :]
-    new_keys = ag[own_head, own_rows:, :]
-    new_values = ag[kv_heads + own_head, own_rows:, :]
-    new_rows = ag.shape[1] - own_rows
+    own_q = ag[core, chip, 0:own_rows, :]
+    new_keys = ag[lax.rem(own_head, 2), own_head // 2, own_rows:, :]
+    new_values = ag[lax.rem(kv_heads + own_head, 2), (kv_heads + own_head) // 2, own_rows:, :]
+    new_rows = ag.shape[2] - own_rows
     scores = lax.dot_general(own_q, new_keys, (((1,), (1,)), ((), ())), preferred_element_type=f32)
     scores = scores * score_scale
     row = lax.broadcasted_iota(jnp.int32, (own_rows, new_rows), 0)
@@ -464,20 +487,22 @@
 
     half_width = width // 2
 
-    def out_part(i):
-        out_copy(i).wait()
-        part = jnp.dot(attention, o_buf[i], preferred_element_type=f32)
-        return jnp.concatenate([part[:, :half_width], part[:, half_width:]], axis=0)
-
     def o_copy(step, target, source):
         return remote(OUT, o_send.at[step], o_recv.at[source], step, source, target)
 
-    def send_out(step, target):
-        o_send[step] = out_part(step - 1).astype(bf16)
-        o_copy(step, target, me).start()
-
-    each_peer(send_out)
-    result = out_part(n - 1)
+    for group in range(n // GROUP):
+        for i in range(group * GROUP, (group + 1) * GROUP):
+            out_copy(i).wait()
+        whole = jnp.dot(attention, o_buf[group], preferred_element_type=f32)
+        for at in range(GROUP):
+            step = group * GROUP + at + 1
+            begin = at * width
+            result = jnp.concatenate(
+                [whole[:, begin:begin + half_width], whole[:, begin + half_width:begin + width]],
+                axis=0)
+            if step < n:
+                o_send[step] = result.astype(bf16)
+                o_copy(step, peer(step), me).start()
 
     def take_out(step, total):
         source = peer(step)
@@ -491,12 +516,13 @@
 
     def finish(step, target):
         sq_copy(step, target, me).wait_send()
-        ag_copy(step, target, me).wait_send()
         st_copy(step, target, me).wait_send()
         att_copy(step, target, me).wait_send()
         o_copy(step, target, me).wait_send()
 
     each_peer(finish)
+    each_chip(lambda step, target: ag_copy(step, target, chip).wait_send())
+    pair_copy(core).wait_send()
     for j in range(chips):
         sib_copy(j).wait_send()
     for j in range(chips - 1):
@@ -518,12 +544,17 @@
     chips = n // 2
     piece = own_width + head_dim
     f32, bf16 = jnp.float32, jnp.bfloat16
-    smem = pl.BlockSpec(memory_space=pltpu.SMEM)
     vmem = pl.BlockSpec(memory_space=pltpu.VMEM)
     hbm = pl.BlockSpec(memory_space=pltpu.HBM)
     scratch = [
-        pltpu.VMEM((n, width, piece), bf16),
-        pltpu.VMEM((n, own_width, width), bf16),
+        pltpu.SMEM(head_kind.shape, jnp.int32),
+        pltpu.SMEM(cache_len.shape, jnp.int32),
+        pltpu.SMEM(sink_len.shape, jnp.int32),
+        pltpu.SMEM(window_len.shape, jnp.int32),
+        pltpu.VMEM(hidden.shape, bf16),
+        pltpu.VMEM(norm_gain.shape, bf16),
+        pltpu.VMEM((n // GROUP, width, GROUP * piece), bf16),
+        pltpu.VMEM((n // GROUP, own_width, GROUP * width), bf16),
         pltpu.VMEM(ret_keys.shape, bf16),
         pltpu.VMEM(ret_values.shape, bf16),
         pltpu.VMEM(stream_keys.shape, bf16),
@@ -534,7 +565,7 @@
         pltpu.VMEM((chips, tokens, piece), f32),
         pltpu.VMEM((chips, tokens, piece), f32),
         pltpu.VMEM((chips, tokens, piece), f32),
-        pltpu.VMEM((n, own_rows + 16, head_dim), bf16),
+        pltpu.VMEM((2, chips, own_rows + 16, head_dim), bf16),
         pltpu.VMEM((slots, share, own_rows, head_dim), bf16),
         pltpu.VMEM((128, 128), f32),
         pltpu.VMEM((n, own_rows, head_dim), bf16),
@@ -543,6 +574,7 @@
         pltpu.VMEM((n, 1, 128), f32),
         pltpu.VMEM((n, 2 * tokens, width // 2), bf16),
         pltpu.VMEM((n, 2 * tokens, width // 2), bf16),
+        pltpu.SemaphoreType.DMA((6,)),
         pltpu.SemaphoreType.DMA((3, n)),
         pltpu.SemaphoreType.DMA((2, 1 + requests)),
         pltpu.SemaphoreType.DMA((7, n)),
@@ -554,15 +586,15 @@
             jax.ShapeDtypeStruct(hidden.shape, bf16),
             jax.ShapeDtypeStruct((requests, drafts, kv_weight.shape[1]), bf16),
         ),
-        in_specs=[smem] * 4 + [vmem] * 2 + [hbm] * 7,
+        in_specs=[hbm] * 13,
         out_specs=(vmem, vmem),
         scratch_shapes=scratch,
         compiler_params=pltpu.CompilerParams(
-            collective_id=0, has_side_effects=True, vmem_limit_bytes=52 * 2**20
+            collective_id=0, has_side_effects=True, vmem_limit_bytes=62 * 2**20
         ),
         name="decode_step",
     )(
-        head_kind, cache_len, sink_len, window_len, hidden, norm_gain.reshape(1, width),
+        head_kind, cache_len, sink_len, window_len, hidden, norm_gain,
         q_weight, kv_weight, out_weight, ret_keys, ret_values, stream_keys, stream_values,
     )
 
@@ -583,7 +615,7 @@
     kv_heads = head_kind.shape[0]
     heads = own_width // head_dim
     return (
-        n % 2 == 0 and n <= 128 and n % kv_heads == 0 and tokens == 8
+        n % (2 * GROUP) == 0 and n <= 128 and n % kv_heads == 0 and tokens == 8
         and head_dim == 128 and width % 256 == 0 and own_width % head_dim == 0
         and q_weight.shape[1] == n * own_width and kv_weight.shape[1] == n * head_dim
         and n == 2 * kv_heads and power_of_two(heads * drafts) and power_of_two(drafts)

time: 50.7 us -> 46.7 us (0.921)
  local copies, waits for them, and re-layouts: 7.11 us -> 2.68 us
  Pallas kernels: 42.6 us -> 43.2 us
    unnamed x16 -> x2, local copies, waits for them, and re-layouts: 6.43 us -> 2.68 us
    reshape x1 -> x0, local copies, waits for them, and re-layouts: 0.68 us -> none  [fused_device(): norm_gain.reshape(1, width)]
    pallas_call x1, Pallas kernels: 42.6 us -> 43.2 us  [fused_device(): pl.pallas_call(step_kernel, out_shape=(jax.ShapeDtypeStruct(hidden.shape,...]
where the time goes in v2:
time: 46.7 us; the launch traced here: 46.5 us
  Pallas kernels  43.2 us (93%)
  local copies, waits for them, and re-layouts  2.68 us (6%)
  between operations  0.64 us (1%)
    pallas_call x1, Pallas kernels, fused_device(): pl.pallas_call(step_kernel, out_shape=(jax.ShapeDtypeStruct(hidden.shape,...  43.2 us
    unnamed x2, local copies, waits for them, and re-layouts  2.68 us

profile of v2, /device:TPU:0, one launch (start us, length us, event | category | flops | bytes accessed | tf_op | source)
XLA Modules:
  0.0 46.5 jit_solution(6966307062329789353)
XLA Ops:
  0.6 43.2 %decode_step.1 = (bf16[2,4,512]{2,1,0:T(4,128)(2,1)}, bf16[2,4,2048]{2,1,0:T(4,128)(2,1)}) custom-call(s32[8]{0:T(128)} %kind_hbm.1, s32[2]{0:T(128)} %clen_hbm.1, s32[2]{0:T(128)} %slen_hbm.1, s32[2]{0:T(128)} %wlen_hbm.1, bf16[2,4,512]{2,1,0:T(4,128)(2,1)} %hidden_hbm.1, bf16[512]{0:T(512)(128)(2,1)} %gain_hbm.1, bf16[512,8192]{1,0:T(8,128)(2,1)} %qw_hbm.1, ...), custom_call_target="tpu_custom_call" | custom-call | tf_op jit(solution)/shard_map/decode_step/pallas_call | solution.py:583
  43.8 1.3 %copy.17 = bf16[2,4,512]{2,1,0:T(4,128)(2,1)} copy(bf16[2,4,512]{2,1,0:T(4,128)(2,1)} %get-tuple-element.4) | data formatting | bytes 16384
  45.1 1.4 %copy.18 = bf16[2,4,2048]{2,1,0:T(4,128)(2,1)} copy(bf16[2,4,2048]{2,1,0:T(4,128)(2,1)} %get-tuple-element.5) | data formatting | bytes 65536

commit v3 on v2

--- a/solution.py
+++ b/solution.py
@@ -220,35 +220,35 @@
         return lax.rem(me + step, n)
 
     def each_peer(body):
-        def run(step, carry):
+        for step in range(1, n):
             body(step, peer(step))
-            return carry
-        lax.fori_loop(1, n, run, 0)
-
-    def chunk_owner(i):
-        target_chip = lax.rem(chip + 1 + i % chips, chips)
-        return 2 * target_chip + (1 - core if i < chips else core)
-
-    def weight_copies(i):
-        p = chunk_owner(i)
-        qcols = pl.ds(pl.multiple_of(p * own_width, own_width), own_width)
-        kcols = pl.ds(pl.multiple_of(p * head_dim, head_dim), head_dim)
-        at = (i % GROUP) * piece
+
+    def arrived(buffer, sem):
+        span = buffer.at[pl.ds(1, n - 1)]
+        pltpu.make_async_copy(span, span, sem).wait()
+
+    slabs = n // GROUP
+    own_slab = me // GROUP
+
+    def slab(k):
+        return lax.rem(own_slab + 1 + k, slabs)
+
+    def columns(k, size):
+        return pl.ds(pl.multiple_of(slab(k) * (GROUP * size), GROUP * size), GROUP * size)
+
+    def weight_copies(k):
         return (
             pltpu.make_async_copy(
-                qw_hbm.at[:, qcols], w_buf.at[i // GROUP, :, pl.ds(at, own_width)],
-                load_sem.at[0, i]),
+                qw_hbm.at[:, columns(k, own_width)],
+                w_buf.at[k, :, pl.ds(0, GROUP * own_width)], load_sem.at[0, k]),
             pltpu.make_async_copy(
-                kvw_hbm.at[:, kcols], w_buf.at[i // GROUP, :, pl.ds(at + own_width, head_dim)],
-                load_sem.at[1, i]),
+                kvw_hbm.at[:, columns(k, head_dim)],
+                w_buf.at[k, :, pl.ds(GROUP * own_width, GROUP * head_dim)], load_sem.at[1, k]),
         )
 
-    def out_copy(i):
-        p = lax.rem(me + 1 + i, n)
-        cols = pl.ds(pl.multiple_of(p * width, width), width)
+    def out_copy(k):
         return pltpu.make_async_copy(
-            ow_hbm.at[:, cols], o_buf.at[i // GROUP, :, pl.ds((i % GROUP) * width, width)],
-            load_sem.at[2, i])
+            ow_hbm.at[:, columns(k, width)], o_buf.at[k], load_sem.at[2, k])
 
     small = [
         pltpu.make_async_copy(src, dst, small_sem.at[at]) for at, (src, dst) in enumerate((
@@ -257,13 +257,12 @@
     ]
     for copy in small:
         copy.start()
-    for i in range(n):
-        for copy in weight_copies(i):
-            copy.start()
-
     barrier = pltpu.get_barrier_semaphore()
     each_peer(lambda step, target: pl.semaphore_signal(
         barrier, inc=1, device_id={"seq": target}, device_id_type=MESH))
+    for k in range(slabs):
+        for copy in weight_copies(k):
+            copy.start()
 
     for copy in small:
         copy.wait()
@@ -272,14 +271,14 @@
     eye = (lax.broadcasted_iota(jnp.int32, (tokens, 128), 0)
            == lax.broadcasted_iota(jnp.int32, (tokens, 128), 1))
     sq_send[...] = jnp.sum(jnp.where(eye, squares, 0.0), axis=0, keepdims=True)
-    sq_recv[me] = sq_send[...]
+    sq_recv[0] = sq_send[...]
     stat_cols[...] = jnp.zeros_like(stat_cols)
     pl.semaphore_wait(barrier, n - 1)
 
-    def sq_copy(step, target, source):
-        return remote(SQ, sq_send, sq_recv.at[source], step, source, target)
-
-    each_peer(lambda step, target: sq_copy(step, target, me).start())
+    def sq_copy(step, target):
+        return remote(SQ, sq_send, sq_recv.at[step], 0, 0, target)
+
+    each_peer(lambda step, target: sq_copy(step, target).start())
 
     cache_copies = [
         (pltpu.make_async_copy(sk_hbm, sk, cache_sem.at[0, 0]),
@@ -293,7 +292,7 @@
         for copy in pair:
             copy.start()
 
-    each_peer(lambda step, source: sq_copy(step, source, source).wait_recv())
+    arrived(sq_recv, recv_sem.at[SQ, 0])
     total_row = sq_recv[0]
     for s in range(1, n):
         total_row = total_row + sq_recv[s]
@@ -301,42 +300,70 @@
     inverse = lax.rsqrt(total_sq / (width * n) + epsilon)
     normed = (hidden32 * inverse * gain_ref[...].astype(f32).reshape(1, width)).astype(bf16)
 
-    def project(group):
-        for i in range(group * GROUP, (group + 1) * GROUP):
-            for copy in weight_copies(i):
-                copy.wait()
-        whole = jnp.dot(normed, w_buf[group], preferred_element_type=f32)
-        return [whole[:, at * piece:(at + 1) * piece] for at in range(GROUP)]
-
-    def sib_copy(j):
-        return remote(SIB, sib_send.at[j], sib_recv.at[j], j, j, sibling)
-
-    for group in range(chips // GROUP):
-        for at, value in enumerate(project(group)):
-            sib_send[group * GROUP + at] = value
-        for at in range(GROUP):
-            sib_copy(group * GROUP + at).start()
-
-    def rs_copy(j):
-        target = 2 * lax.rem(chip + 1 + j, chips) + core
-        return remote(RS, rs_send.at[j], rs_recv.at[j], j, j, target)
-
-    for group in range(chips // GROUP):
-        values = project(chips // GROUP + group)
-        for at, value in enumerate(values):
-            j = group * GROUP + at
-            sib_copy(j).wait_recv()
-            own = value + sib_recv[j]
-            if j < chips - 1:
-                rs_send[j] = own
-                rs_copy(j).start()
-
-    for i in range(n):
-        out_copy(i).start()
-
-    for j in range(chips - 1):
-        rs_copy(j).wait_recv()
-        own = own + rs_recv[j]
+    def part(whole, owner):
+        return jnp.concatenate(
+            [whole[:, owner * own_width:(owner + 1) * own_width],
+             whole[:, GROUP * own_width + owner * head_dim:
+                   GROUP * own_width + (owner + 1) * head_dim]], axis=1)
+
+    def pick(flag, first, second):
+        return jnp.where(flag == 0, first, second)
+
+    def sib_copy(k):
+        return remote(SIB, sib_send.at[k], sib_recv.at[k], k, k, sibling)
+
+    pairs = GROUP // 2
+    own_pair = lax.rem(chip, pairs)
+
+    def rs_copy(k, u):
+        target = 2 * (slab(k) * pairs + u) + core
+        return remote(
+            RS, rs_send.at[k * pairs + u], rs_recv.at[k * pairs + own_pair],
+            k * pairs + u, k * pairs + own_pair, target)
+
+    def rs_arrival(k, u):
+        return remote(
+            RS, rs_send.at[0], rs_recv.at[k * pairs + u], 0, k * pairs + u, sibling)
+
+    mine = []
+
+    def send_sums(k):
+        sib_copy(k).wait_recv()
+        for u in range(pairs):
+            rs_send[k * pairs + u] = mine[k][u] + sib_recv[k, u]
+            rs_copy(k, u).start()
+
+    for k in range(slabs):
+        for copy in weight_copies(k):
+            copy.wait()
+        whole = jnp.dot(normed, w_buf[k], preferred_element_type=f32)
+        sides = [(part(whole, 2 * u), part(whole, 2 * u + 1)) for u in range(pairs)]
+        mine.append([pick(core, *side) for side in sides])
+        for u in range(pairs):
+            sib_send[k, u] = pick(core, sides[u][1], sides[u][0])
+        sib_copy(k).start()
+        if k > 0:
+            send_sums(k - 1)
+
+    last = slabs - 1
+    sib_copy(last).wait_recv()
+    for u in range(pairs):
+        rs_send[last * pairs + u] = mine[last][u] + sib_recv[last, u]
+    for hop in range(1, pairs):
+        rs_copy(last, lax.rem(own_pair + hop, pairs)).start()
+    own = rs_send[last * pairs + own_pair]
+
+    for k in range(slabs):
+        out_copy(k).start()
+
+    for k in range(last):
+        for u in range(pairs):
+            rs_arrival(k, u).wait_recv()
+            own = own + rs_recv[k * pairs + u]
+    for hop in range(1, pairs):
+        u = lax.rem(own_pair + hop, pairs)
+        rs_arrival(last, u).wait_recv()
+        own = own + rs_recv[last * pairs + u]
 
     def by_head(values):
         return jnp.concatenate(
@@ -353,10 +380,8 @@
             AG, ag.at[core, source], ag.at[core, source], step, source, 2 * target + core)
 
     def each_chip(body):
-        def run(step, carry):
+        for step in range(1, chips):
             body(step, lax.rem(chip + step, chips))
-            return carry
-        lax.fori_loop(1, chips, run, 0)
 
     def pair_copy(side):
         return remote(AG, ag.at[side], ag.at[side], chips, chips, sibling)
@@ -385,11 +410,13 @@
         for b in range(requests):
             new_ref[b, :, p * head_dim:(p + 1) * head_dim] = entries[b * drafts:(b + 1) * drafts]
 
-    def attend(b, j, keys, values, visible):
+    def score(b, j, keys):
         q = jnp.concatenate(
             [ag[s % 2, head_of[j] * share // 2 + s // 2, b * half_rows:(b + 1) * half_rows, :]
              for s in range(share)], axis=0)
-        scores = lax.dot_general(q, keys, (((1,), (1,)), ((), ())), preferred_element_type=f32)
+        return lax.dot_general(q, keys, (((1,), (1,)), ((), ())), preferred_element_type=f32)
+
+    def attend(b, j, scores, values, visible):
         scores = jnp.where(visible, scores, floor_score)
         peak = jnp.max(scores, axis=-1, keepdims=True)
         weights = jnp.exp2((scores - peak) * exp_scale)
@@ -415,34 +442,39 @@
     for b in range(requests):
         seen = (slot_pos < slen_ref[b]) | (
             (slot_pos >= SINK_CAP) & (slot_pos < SINK_CAP + wlen_ref[b]))
+        later = score(b, retrieval, sk[b, 0])
         for r in range(running):
-            attend(b, retrieval + r, sk[b, r], sv[b, r], seen)
+            scores = later
+            if r + 1 < running:
+                later = score(b, retrieval + r + 1, sk[b, r + 1])
+            attend(b, retrieval + r, scores, sv[b, r], seen)
     for b in range(requests):
         for copy in cache_copies[1 + b]:
             copy.wait()
         seen = cache_pos < clen_ref[b]
+        later = score(b, 0, rk[b, 0])
         for r in range(retrieval):
-            attend(b, r, rk[b, r], rv[b, r], seen)
+            scores = later
+            if r + 1 < retrieval:
+                later = score(b, r + 1, rk[b, r + 1])
+            attend(b, r, scores, rv[b, r], seen)
 
     stat_rows = stat_cols[...].T
     for p in range(n):
         st_send[p] = stat_rows[p:p + 1, :]
     for g in range(kv_heads):
         a_send[g * share:(g + 1) * share] = a_res[slot_of[g]]
-    st_recv[me] = st_send[me]
-    a_recv[me] = a_send[me]
-
-    def att_copy(step, target, source):
-        return remote(ATT, a_send.at[target], a_recv.at[source], step, source, target)
-
-    def st_copy(step, target, source):
-        return remote(STAT, st_send.at[target], st_recv.at[source], step, source, target)
-
-    def send_attention(step, target):
-        st_copy(step, target, me).start()
-        att_copy(step, target, me).start()
-
-    each_peer(send_attention)
+    st_recv[0] = st_send[me]
+    a_recv[0] = a_send[me]
+
+    def att_copy(step, target):
+        return remote(ATT, a_send.at[target], a_recv.at[step], 0, 0, target)
+
+    def st_copy(step, target):
+        return remote(STAT, st_send.at[target], st_recv.at[step], 0, 0, target)
+
+    each_peer(lambda step, target: st_copy(step, target).start())
+    each_peer(lambda step, target: att_copy(step, target).start())
 
     own_head = me // share
     own_q = ag[core, chip, 0:own_rows, :]
@@ -462,11 +494,7 @@
     new_total = jnp.sum(new_weights, axis=-1, keepdims=True)
     new_out = jnp.dot(new_weights.astype(bf16), new_values, preferred_element_type=f32)
 
-    def wait_attention(step, source):
-        st_copy(step, source, source).wait_recv()
-        att_copy(step, source, source).wait_recv()
-
-    each_peer(wait_attention)
+    arrived(st_recv, recv_sem.at[STAT, 0])
     stats = jnp.concatenate(
         [st_recv[s] for s in range(n)] + [jnp.zeros((128 - n, 128), f32)], axis=0).T
     lane = lax.broadcasted_iota(jnp.int32, (own_rows, 128), 1)
@@ -477,6 +505,7 @@
     new_factor = jnp.exp(new_peak - top)
     denominator = jnp.sum(factors * totals, axis=-1, keepdims=True) + new_factor * new_total
     numerator = new_factor * new_out
+    arrived(a_recv, recv_sem.at[ATT, 0])
     for s in range(n):
         numerator = numerator + factors[:, s:s + 1] * a_recv[s].astype(f32)
     attended = numerator / denominator
@@ -487,46 +516,58 @@
 
     half_width = width // 2
 
-    def o_copy(step, target, source):
-        return remote(OUT, o_send.at[step], o_recv.at[source], step, source, target)
-
-    for group in range(n // GROUP):
-        for i in range(group * GROUP, (group + 1) * GROUP):
-            out_copy(i).wait()
-        whole = jnp.dot(attention, o_buf[group], preferred_element_type=f32)
+    def o_copy(k, at):
+        owner = slab(k) * GROUP + at
+        slot = k * GROUP + lax.rem(me, GROUP)
+        return remote(OUT, o_send.at[k * GROUP + at], o_recv.at[slot], k * GROUP + at, slot, owner)
+
+    def o_arrival(k, at):
+        slot = k * GROUP + at
+        return remote(OUT, o_send.at[0], o_recv.at[slot], 0, slot, sibling)
+
+    own_at = lax.rem(me, GROUP)
+    for k in range(slabs):
+        out_copy(k).wait()
+        whole = jnp.dot(attention, o_buf[k], preferred_element_type=f32)
         for at in range(GROUP):
-            step = group * GROUP + at + 1
             begin = at * width
-            result = jnp.concatenate(
+            o_send[k * GROUP + at] = jnp.concatenate(
                 [whole[:, begin:begin + half_width], whole[:, begin + half_width:begin + width]],
-                axis=0)
-            if step < n:
-                o_send[step] = result.astype(bf16)
-                o_copy(step, peer(step), me).start()
-
-    def take_out(step, total):
-        source = peer(step)
-        o_copy(step, source, source).wait_recv()
-        return total + o_recv[source].astype(f32)
-
-    result = lax.fori_loop(1, n, take_out, result)
+                axis=0).astype(bf16)
+            if k < slabs - 1:
+                o_copy(k, at).start()
+    for hop in range(1, GROUP):
+        o_copy(slabs - 1, lax.rem(own_at + hop, GROUP)).start()
+    result = o_send[(slabs - 1) * GROUP + own_at].astype(f32)
+    for k in range(slabs):
+        for at in range(GROUP):
+            if k < slabs - 1:
+                o_arrival(k, at).wait_recv()
+                result = result + o_recv[k * GROUP + at].astype(f32)
+            elif at > 0:
+                place = lax.rem(own_at + at, GROUP)
+                o_arrival(k, place).wait_recv()
+                result = result + o_recv[k * GROUP + place].astype(f32)
     result = jnp.concatenate([result[:tokens], result[tokens:]], axis=1).astype(bf16)
     for b in range(requests):
         out_ref[b] = result[b * drafts:(b + 1) * drafts]
 
-    def finish(step, target):
-        sq_copy(step, target, me).wait_send()
-        st_copy(step, target, me).wait_send()
-        att_copy(step, target, me).wait_send()
-        o_copy(step, target, me).wait_send()
-
-    each_peer(finish)
+    arrived(sq_recv, send_sem.at[SQ, 0])
+    arrived(st_recv, send_sem.at[STAT, 0])
+    arrived(a_recv, send_sem.at[ATT, 0])
     each_chip(lambda step, target: ag_copy(step, target, chip).wait_send())
     pair_copy(core).wait_send()
-    for j in range(chips):
-        sib_copy(j).wait_send()
-    for j in range(chips - 1):
-        rs_copy(j).wait_send()
+    for k in range(slabs):
+        sib_copy(k).wait_send()
+        if k < last:
+            for u in range(pairs):
+                rs_copy(k, u).wait_send()
+            for at in range(GROUP):
+                o_copy(k, at).wait_send()
+    for hop in range(1, pairs):
+        rs_copy(last, lax.rem(own_pair + hop, pairs)).wait_send()
+    for hop in range(1, GROUP):
+        o_copy(last, lax.rem(own_at + hop, GROUP)).wait_send()
 
 
 def fused_device(
@@ -561,8 +602,8 @@
         pltpu.VMEM(stream_values.shape, bf16),
         pltpu.VMEM((1, 128), f32),
         pltpu.VMEM((n, 1, 128), f32),
-        pltpu.VMEM((chips, tokens, piece), f32),
-        pltpu.VMEM((chips, tokens, piece), f32),
+        pltpu.VMEM((n // GROUP, GROUP // 2, tokens, piece), f32),
+        pltpu.VMEM((n // GROUP, GROUP // 2, tokens, piece), f32),
         pltpu.VMEM((chips, tokens, piece), f32),
         pltpu.VMEM((chips, tokens, piece), f32),
         pltpu.VMEM((2, chips, own_rows + 16, head_dim), bf16),

time: 46.7 us -> 42.8 us (0.916)
  Pallas kernels: 43.2 us -> 39.2 us
    pallas_call x1, Pallas kernels: 43.2 us -> 39.2 us  [fused_device(): pl.pallas_call(step_kernel, out_shape=(jax.ShapeDtypeStruct(hidden.shape,...]
where the time goes in v3:
time: 42.8 us; the launch traced here: 42.5 us
  Pallas kernels  39.2 us (92%)
  local copies, waits for them, and re-layouts  2.68 us (6%)
  between operations  0.64 us (1%)
    pallas_call x1, Pallas kernels, fused_device(): pl.pallas_call(step_kernel, out_shape=(jax.ShapeDtypeStruct(hidden.shape,...  39.2 us
    unnamed x2, local copies, waits for them, and re-layouts  2.68 us

profile of v3, /device:TPU:0, one launch (start us, length us, event | category | flops | bytes accessed | tf_op | source)
XLA Modules:
  0.0 42.5 jit_solution(15830295081242127307)
XLA Ops:
  0.6 39.2 %decode_step.1 = (bf16[2,4,512]{2,1,0:T(4,128)(2,1)}, bf16[2,4,2048]{2,1,0:T(4,128)(2,1)}) custom-call(s32[8]{0:T(128)} %kind_hbm.1, s32[2]{0:T(128)} %clen_hbm.1, s32[2]{0:T(128)} %slen_hbm.1, s32[2]{0:T(128)} %wlen_hbm.1, bf16[2,4,512]{2,1,0:T(4,128)(2,1)} %hidden_hbm.1, bf16[512]{0:T(512)(128)(2,1)} %gain_hbm.1, bf16[512,8192]{1,0:T(8,128)(2,1)} %qw_hbm.1, ...), custom_call_target="tpu_custom_call" | custom-call | tf_op jit(solution)/shard_map/decode_step/pallas_call | solution.py:624
  39.9 1.3 %copy.17 = bf16[2,4,512]{2,1,0:T(4,128)(2,1)} copy(bf16[2,4,512]{2,1,0:T(4,128)(2,1)} %get-tuple-element.4) | data formatting | bytes 16384
  41.2 1.4 %copy.18 = bf16[2,4,2048]{2,1,0:T(4,128)(2,1)} copy(bf16[2,4,2048]{2,1,0:T(4,128)(2,1)} %get-tuple-element.5) | data formatting | bytes 65536

commit v4 on v3

--- a/solution.py
+++ b/solution.py
@@ -207,7 +207,7 @@
     group_rows = share * half_rows
     score_scale = head_dim ** (-0.5)
     exp_scale = score_scale * math.log2(math.e)
-    SQ, SIB, RS, AG, ATT, STAT, OUT = range(7)
+    SQ, SIB, RS, AG, STAT, OUT, ATT = range(7)
 
     def remote(kind, src, dst, send_slot, recv_slot, target):
         return pltpu.make_async_remote_copy(
@@ -416,22 +416,29 @@
              for s in range(share)], axis=0)
         return lax.dot_general(q, keys, (((1,), (1,)), ((), ())), preferred_element_type=f32)
 
-    def attend(b, j, scores, values, visible):
-        scores = jnp.where(visible, scores, floor_score)
-        peak = jnp.max(scores, axis=-1, keepdims=True)
-        weights = jnp.exp2((scores - peak) * exp_scale)
-        total = jnp.sum(weights, axis=-1, keepdims=True)
-        block = jnp.dot(weights.astype(bf16), values, preferred_element_type=f32)
-        a_res[j, :, b * half_rows:(b + 1) * half_rows, :] = block.astype(bf16).reshape(
-            share, half_rows, head_dim)
+    def attend(parts):
+        scores = [jnp.where(seen, score(b, j, keys), floor_score)
+                  for b, j, keys, _, seen in parts]
+        peaks = [jnp.max(found, axis=-1, keepdims=True) for found in scores]
+        weights = [jnp.exp2((found - peak) * exp_scale) for found, peak in zip(scores, peaks)]
+        totals = [jnp.sum(weight, axis=-1, keepdims=True) for weight in weights]
+        blocks = [jnp.dot(weight.astype(bf16), part[3], preferred_element_type=f32)
+                  for weight, part in zip(weights, parts)]
+        for part, block in zip(parts, blocks):
+            b, j = part[0], part[1]
+            a_res[j, :, b * half_rows:(b + 1) * half_rows, :] = block.astype(bf16).reshape(
+                share, half_rows, head_dim)
         lane = lax.broadcasted_iota(jnp.int32, (half_rows, 128), 1)
-        for at, column in ((0, peak * score_scale), (own_rows, total)):
-            rows = pl.ds(at + b * half_rows, half_rows)
-            kept = stat_cols[rows, :]
-            for s in range(share):
-                kept = jnp.where(lane == share * head_of[j] + s,
-                                 column[s * half_rows:(s + 1) * half_rows], kept)
-            stat_cols[rows, :] = kept
+        for b in sorted({part[0] for part in parts}):
+            for at, columns_of in ((0, peaks), (own_rows, totals)):
+                rows = pl.ds(at + b * half_rows, half_rows)
+                kept = stat_cols[rows, :]
+                for part, column in zip(parts, columns_of):
+                    if part[0] == b:
+                        for s in range(share):
+                            kept = jnp.where(lane == share * head_of[part[1]] + s,
+                                             column[s * half_rows:(s + 1) * half_rows], kept)
+                stat_cols[rows, :] = kept
 
     for copy in cache_copies[0]:
         copy.wait()
@@ -439,42 +446,41 @@
     slot_pos = me * slots + lax.broadcasted_iota(jnp.int32, (1, slots), 1)
     positions = rk.shape[2]
     cache_pos = me * positions + lax.broadcasted_iota(jnp.int32, (1, positions), 1)
+    small_parts = []
     for b in range(requests):
         seen = (slot_pos < slen_ref[b]) | (
             (slot_pos >= SINK_CAP) & (slot_pos < SINK_CAP + wlen_ref[b]))
-        later = score(b, retrieval, sk[b, 0])
         for r in range(running):
-            scores = later
-            if r + 1 < running:
-                later = score(b, retrieval + r + 1, sk[b, r + 1])
-            attend(b, retrieval + r, scores, sv[b, r], seen)
+            small_parts.append((b, retrieval + r, sk[b, r], sv[b, r], seen))
+    attend(small_parts)
+
+    def att_copy(b, step, target):
+        rows = pl.ds(b * half_rows, half_rows)
+        return remote(ATT + b, a_send.at[target, rows], a_recv.at[step, rows], 0, 0, target)
+
     for b in range(requests):
         for copy in cache_copies[1 + b]:
             copy.wait()
         seen = cache_pos < clen_ref[b]
-        later = score(b, 0, rk[b, 0])
-        for r in range(retrieval):
-            scores = later
-            if r + 1 < retrieval:
-                later = score(b, r + 1, rk[b, r + 1])
-            attend(b, r, scores, rv[b, r], seen)
-
-    stat_rows = stat_cols[...].T
+        attend([(b, r, rk[b, r], rv[b, r], seen) for r in range(retrieval)])
+        rows = slice(b * half_rows, (b + 1) * half_rows)
+        for g in range(kv_heads):
+            a_send[g * share:(g + 1) * share, rows] = a_res[slot_of[g], :, rows]
+        a_recv[0, rows] = a_send[me, rows]
+        if b < requests - 1:
+            each_peer(lambda step, target: att_copy(b, step, target).start())
+
+    lane = lax.broadcasted_iota(jnp.int32, (128, 128), 0)
+    stat_rows = jnp.where(lane < own_rows, stat_cols[...] * score_scale, stat_cols[...]).T
     for p in range(n):
         st_send[p] = stat_rows[p:p + 1, :]
-    for g in range(kv_heads):
-        a_send[g * share:(g + 1) * share] = a_res[slot_of[g]]
     st_recv[0] = st_send[me]
-    a_recv[0] = a_send[me]
-
-    def att_copy(step, target):
-        return remote(ATT, a_send.at[target], a_recv.at[step], 0, 0, target)
 
     def st_copy(step, target):
         return remote(STAT, st_send.at[target], st_recv.at[step], 0, 0, target)
 
     each_peer(lambda step, target: st_copy(step, target).start())
-    each_peer(lambda step, target: att_copy(step, target).start())
+    each_peer(lambda step, target: att_copy(requests - 1, step, target).start())
 
     own_head = me // share
     own_q = ag[core, chip, 0:own_rows, :]
@@ -505,7 +511,8 @@
     new_factor = jnp.exp(new_peak - top)
     denominator = jnp.sum(factors * totals, axis=-1, keepdims=True) + new_factor * new_total
     numerator = new_factor * new_out
-    arrived(a_recv, recv_sem.at[ATT, 0])
+    for b in range(requests):
+        arrived(a_recv.at[:, pl.ds(b * half_rows, half_rows)], recv_sem.at[ATT + b, 0])
     for s in range(n):
         numerator = numerator + factors[:, s:s + 1] * a_recv[s].astype(f32)
     attended = numerator / denominator
@@ -554,7 +561,8 @@
 
     arrived(sq_recv, send_sem.at[SQ, 0])
     arrived(st_recv, send_sem.at[STAT, 0])
-    arrived(a_recv, send_sem.at[ATT, 0])
+    for b in range(requests):
+        arrived(a_recv.at[:, pl.ds(b * half_rows, half_rows)], send_sem.at[ATT + b, 0])
     each_chip(lambda step, target: ag_copy(step, target, chip).wait_send())
     pair_copy(core).wait_send()
     for k in range(slabs):
@@ -618,14 +626,14 @@
         pltpu.SemaphoreType.DMA((6,)),
         pltpu.SemaphoreType.DMA((3, n)),
         pltpu.SemaphoreType.DMA((2, 1 + requests)),
-        pltpu.SemaphoreType.DMA((7, n)),
-        pltpu.SemaphoreType.DMA((7, n)),
+        pltpu.SemaphoreType.DMA((6 + requests, n)),
+        pltpu.SemaphoreType.DMA((6 + requests, n)),
     ]
     return pl.pallas_call(
         step_kernel,
         out_shape=(
-            jax.ShapeDtypeStruct(hidden.shape, bf16),
-            jax.ShapeDtypeStruct((requests, drafts, kv_weight.shape[1]), bf16),
+            pltpu.VMEM(hidden.shape, bf16),
+            pltpu.VMEM((requests, drafts, kv_weight.shape[1]), bf16),
         ),
         in_specs=[hbm] * 13,
         out_specs=(vmem, vmem),

time: 42.8 us -> 39.1 us (0.914)
  Pallas kernels: 39.2 us -> 37 us
  local copies, waits for them, and re-layouts: 2.68 us -> 1.22 us
    pallas_call x1, Pallas kernels: 39.2 us -> 37 us  [fused_device(): pl.pallas_call(step_kernel, out_shape=(pltpu.VMEM(hidden.shape, bf16), pl...]
    unnamed x2, local copies, waits for them, and re-layouts: 2.68 us -> 1.22 us
where the time goes in v4:
time: 39.1 us; the launch traced here: 38.9 us
  Pallas kernels  37 us (95%)
  local copies, waits for them, and re-layouts  1.22 us (3%)
  between operations  0.64 us (2%)
    pallas_call x1, Pallas kernels, fused_device(): pl.pallas_call(step_kernel, out_shape=(pltpu.VMEM(hidden.shape, bf16), pl...  37 us
    unnamed x2, local copies, waits for them, and re-layouts  1.22 us

profile of v4, /device:TPU:0, one launch (start us, length us, event | category | flops | bytes accessed | tf_op | source)
XLA Modules:
  0.0 38.9 jit_solution(3219880090080793920)
XLA Ops:
  0.6 37.0 %decode_step.1 = (bf16[2,4,512]{2,1,0:T(4,128)(2,1)S(1)}, bf16[2,4,2048]{2,1,0:T(4,128)(2,1)S(1)}) custom-call(s32[8]{0:T(128)} %kind_hbm.1, s32[2]{0:T(128)} %clen_hbm.1, s32[2]{0:T(128)} %slen_hbm.1, s32[2]{0:T(128)} %wlen_hbm.1, bf16[2,4,512]{2,1,0:T(4,128)(2,1)} %hidden_hbm.1, bf16[512]{0:T(512)(128)(2,1)} %gain_hbm.1, bf16[512,8192]{1,0:T(8,128)(2,1)} %qw_hbm.1, ...), custom_call_target="tpu_custom_call" | custom-call | tf_op jit(solution)/shard_map/decode_step/pallas_call | solution.py:632
  37.7 0.6 %copy.17 = bf16[2,4,512]{2,1,0:T(4,128)(2,1)} copy(bf16[2,4,512]{2,1,0:T(4,128)(2,1)S(1)} %get-tuple-element.2) | data formatting | bytes 16384
  38.3 0.6 %copy.18 = bf16[2,4,2048]{2,1,0:T(4,128)(2,1)} copy(bf16[2,4,2048]{2,1,0:T(4,128)(2,1)S(1)} %get-tuple-element.3) | data formatting | bytes 65536

commit v5 on v4

--- a/solution.py
+++ b/solution.py
@@ -184,7 +184,7 @@
     out_ref, new_ref,
     kind_ref, clen_ref, slen_ref, wlen_ref, hidden_ref, gain_ref,
     w_buf, o_buf, rk, rv, sk, sv,
-    sq_send, sq_recv, sib_send, sib_recv, rs_send, rs_recv, ag,
+    sq_send, sq_recv, sib_send, sib_recv, quad_send, quad_recv, rs_send, rs_recv, ag,
     a_res, stat_cols, a_send, a_recv, st_send, st_recv, o_send, o_recv,
     small_sem, load_sem, cache_sem, send_sem, recv_sem,
 ):
@@ -207,7 +207,7 @@
     group_rows = share * half_rows
     score_scale = head_dim ** (-0.5)
     exp_scale = score_scale * math.log2(math.e)
-    SQ, SIB, RS, AG, STAT, OUT, ATT = range(7)
+    SQ, SIB, RS, AG, STAT, OUT, QUAD, ATT = range(8)
 
     def remote(kind, src, dst, send_slot, recv_slot, target):
         return pltpu.make_async_remote_copy(
@@ -288,10 +288,6 @@
         cache_copies.append(
             (pltpu.make_async_copy(rk_hbm.at[b], rk.at[b], cache_sem.at[0, 1 + b]),
              pltpu.make_async_copy(rv_hbm.at[b], rv.at[b], cache_sem.at[1, 1 + b])))
-    for pair in cache_copies:
-        for copy in pair:
-            copy.start()
-
     arrived(sq_recv, recv_sem.at[SQ, 0])
     total_row = sq_recv[0]
     for s in range(1, n):
@@ -325,6 +321,17 @@
         return remote(
             RS, rs_send.at[0], rs_recv.at[k * pairs + u], 0, k * pairs + u, sibling)
 
+    own_at = lax.rem(me, GROUP)
+    last = slabs - 1
+    others = [lax.rem(own_at + hop, GROUP) for hop in range(1, GROUP)]
+
+    def quad_copy(at):
+        return remote(
+            QUAD, quad_send.at[at], quad_recv.at[own_at], at, own_at, own_slab * GROUP + at)
+
+    def quad_arrival(at):
+        return remote(QUAD, quad_send.at[0], quad_recv.at[at], 0, at, sibling)
+
     mine = []
 
     def send_sums(k):
@@ -337,21 +344,25 @@
         for copy in weight_copies(k):
             copy.wait()
         whole = jnp.dot(normed, w_buf[k], preferred_element_type=f32)
-        sides = [(part(whole, 2 * u), part(whole, 2 * u + 1)) for u in range(pairs)]
-        mine.append([pick(core, *side) for side in sides])
-        for u in range(pairs):
-            sib_send[k, u] = pick(core, sides[u][1], sides[u][0])
-        sib_copy(k).start()
+        if k == 1:
+            for pair in cache_copies:
+                for copy in pair:
+                    copy.start()
+        if k < last:
+            sides = [(part(whole, 2 * u), part(whole, 2 * u + 1)) for u in range(pairs)]
+            mine.append([pick(core, *side) for side in sides])
+            for u in range(pairs):
+                sib_send[k, u] = pick(core, sides[u][1], sides[u][0])
+            sib_copy(k).start()
+        else:
+            for at in range(GROUP):
+                quad_send[at] = part(whole, at)
+            for at in others:
+                quad_copy(at).start()
         if k > 0:
             send_sums(k - 1)
 
-    last = slabs - 1
-    sib_copy(last).wait_recv()
-    for u in range(pairs):
-        rs_send[last * pairs + u] = mine[last][u] + sib_recv[last, u]
-    for hop in range(1, pairs):
-        rs_copy(last, lax.rem(own_pair + hop, pairs)).start()
-    own = rs_send[last * pairs + own_pair]
+    own = quad_send[own_at]
 
     for k in range(slabs):
         out_copy(k).start()
@@ -360,10 +371,9 @@
         for u in range(pairs):
             rs_arrival(k, u).wait_recv()
             own = own + rs_recv[k * pairs + u]
-    for hop in range(1, pairs):
-        u = lax.rem(own_pair + hop, pairs)
-        rs_arrival(last, u).wait_recv()
-        own = own + rs_recv[last * pairs + u]
+    for at in others:
+        quad_arrival(at).wait_recv()
+        own = own + quad_recv[at]
 
     def by_head(values):
         return jnp.concatenate(
@@ -532,7 +542,6 @@
         slot = k * GROUP + at
         return remote(OUT, o_send.at[0], o_recv.at[slot], 0, slot, sibling)
 
-    own_at = lax.rem(me, GROUP)
     for k in range(slabs):
         out_copy(k).wait()
         whole = jnp.dot(attention, o_buf[k], preferred_element_type=f32)
@@ -565,15 +574,14 @@
         arrived(a_recv.at[:, pl.ds(b * half_rows, half_rows)], send_sem.at[ATT + b, 0])
     each_chip(lambda step, target: ag_copy(step, target, chip).wait_send())
     pair_copy(core).wait_send()
-    for k in range(slabs):
+    for k in range(last):
         sib_copy(k).wait_send()
-        if k < last:
-            for u in range(pairs):
-                rs_copy(k, u).wait_send()
-            for at in range(GROUP):
-                o_copy(k, at).wait_send()
-    for hop in range(1, pairs):
-        rs_copy(last, lax.rem(own_pair + hop, pairs)).wait_send()
+        for u in range(pairs):
+            rs_copy(k, u).wait_send()
+        for at in range(GROUP):
+            o_copy(k, at).wait_send()
+    for at in others:
+        quad_copy(at).wait_send()
     for hop in range(1, GROUP):
         o_copy(last, lax.rem(own_at + hop, GROUP)).wait_send()
 
@@ -610,8 +618,10 @@
         pltpu.VMEM(stream_values.shape, bf16),
         pltpu.VMEM((1, 128), f32),
         pltpu.VMEM((n, 1, 128), f32),
-        pltpu.VMEM((n // GROUP, GROUP // 2, tokens, piece), f32),
-        pltpu.VMEM((n // GROUP, GROUP // 2, tokens, piece), f32),
+        pltpu.VMEM((n // GROUP - 1, GROUP // 2, tokens, piece), f32),
+        pltpu.VMEM((n // GROUP - 1, GROUP // 2, tokens, piece), f32),
+        pltpu.VMEM((GROUP, tokens, piece), f32),
+        pltpu.VMEM((GROUP, tokens, piece), f32),
         pltpu.VMEM((chips, tokens, piece), f32),
         pltpu.VMEM((chips, tokens, piece), f32),
         pltpu.VMEM((2, chips, own_rows + 16, head_dim), bf16),
@@ -626,8 +636,8 @@
         pltpu.SemaphoreType.DMA((6,)),
         pltpu.SemaphoreType.DMA((3, n)),
         pltpu.SemaphoreType.DMA((2, 1 + requests)),
-        pltpu.SemaphoreType.DMA((6 + requests, n)),
-        pltpu.SemaphoreType.DMA((6 + requests, n)),
+        pltpu.SemaphoreType.DMA((7 + requests, n)),
+        pltpu.SemaphoreType.DMA((7 + requests, n)),
     ]
     return pl.pallas_call(
         step_kernel,

time: 39.1 us -> 39.4 us (level)
  no operation moved by 1% of the time
where the time goes in v5:
time: 39.4 us; the launch traced here: 39.2 us
  Pallas kernels  37.3 us (95%)
  local copies, waits for them, and re-layouts  1.22 us (3%)
  between operations  0.64 us (2%)
    pallas_call x1, Pallas kernels, fused_device(): pl.pallas_call(step_kernel, out_shape=(pltpu.VMEM(hidden.shape, bf16), pl...  37.3 us
    unnamed x2, local copies, waits for them, and re-layouts  1.22 us

profile of v5, /device:TPU:0, one launch (start us, length us, event | category | flops | bytes accessed | tf_op | source)
XLA Modules:
  0.0 39.2 jit_solution(5028533298394945156)
XLA Ops:
  0.6 37.3 %decode_step.1 = (bf16[2,4,512]{2,1,0:T(4,128)(2,1)S(1)}, bf16[2,4,2048]{2,1,0:T(4,128)(2,1)S(1)}) custom-call(s32[8]{0:T(128)} %kind_hbm.1, s32[2]{0:T(128)} %clen_hbm.1, s32[2]{0:T(128)} %slen_hbm.1, s32[2]{0:T(128)} %wlen_hbm.1, bf16[2,4,512]{2,1,0:T(4,128)(2,1)} %hidden_hbm.1, bf16[512]{0:T(512)(128)(2,1)} %gain_hbm.1, bf16[512,8192]{1,0:T(8,128)(2,1)} %qw_hbm.1, ...), custom_call_target="tpu_custom_call" | custom-call | tf_op jit(solution)/shard_map/decode_step/pallas_call | solution.py:642
  38.0 0.6 %copy.17 = bf16[2,4,512]{2,1,0:T(4,128)(2,1)} copy(bf16[2,4,512]{2,1,0:T(4,128)(2,1)S(1)} %get-tuple-element.2) | data formatting | bytes 16384
  38.6 0.6 %copy.18 = bf16[2,4,2048]{2,1,0:T(4,128)(2,1)} copy(bf16[2,4,2048]{2,1,0:T(4,128)(2,1)S(1)} %get-tuple-element.3) | data formatting | bytes 65536

commit v6 on v5

--- a/solution.py
+++ b/solution.py
@@ -288,6 +288,9 @@
         cache_copies.append(
             (pltpu.make_async_copy(rk_hbm.at[b], rk.at[b], cache_sem.at[0, 1 + b]),
              pltpu.make_async_copy(rv_hbm.at[b], rv.at[b], cache_sem.at[1, 1 + b])))
+    for pair in cache_copies:
+        for copy in pair:
+            copy.start()
     arrived(sq_recv, recv_sem.at[SQ, 0])
     total_row = sq_recv[0]
     for s in range(1, n):
@@ -344,10 +347,6 @@
         for copy in weight_copies(k):
             copy.wait()
         whole = jnp.dot(normed, w_buf[k], preferred_element_type=f32)
-        if k == 1:
-            for pair in cache_copies:
-                for copy in pair:
-                    copy.start()
         if k < last:
             sides = [(part(whole, 2 * u), part(whole, 2 * u + 1)) for u in range(pairs)]
             mine.append([pick(core, *side) for side in sides])

time: 39.4 us -> 39.4 us (level)
  no operation moved by 1% of the time
where the time goes in v6:
time: 39.4 us; the launch traced here: 39.2 us
  Pallas kernels  37.3 us (95%)
  local copies, waits for them, and re-layouts  1.22 us (3%)
  between operations  0.64 us (2%)
    pallas_call x1, Pallas kernels, fused_device(): pl.pallas_call(step_kernel, out_shape=(pltpu.VMEM(hidden.shape, bf16), pl...  37.3 us
    unnamed x2, local copies, waits for them, and re-layouts  1.22 us

profile of v6, /device:TPU:0, one launch (start us, length us, event | category | flops | bytes accessed | tf_op | source)
XLA Modules:
  0.0 39.2 jit_solution(1807164835959929801)
XLA Ops:
  0.6 37.3 %decode_step.1 = (bf16[2,4,512]{2,1,0:T(4,128)(2,1)S(1)}, bf16[2,4,2048]{2,1,0:T(4,128)(2,1)S(1)}) custom-call(s32[8]{0:T(128)} %kind_hbm.1, s32[2]{0:T(128)} %clen_hbm.1, s32[2]{0:T(128)} %slen_hbm.1, s32[2]{0:T(128)} %wlen_hbm.1, bf16[2,4,512]{2,1,0:T(4,128)(2,1)} %hidden_hbm.1, bf16[512]{0:T(512)(128)(2,1)} %gain_hbm.1, bf16[512,8192]{1,0:T(8,128)(2,1)} %qw_hbm.1, ...), custom_call_target="tpu_custom_call" | custom-call | tf_op jit(solution)/shard_map/decode_step/pallas_call | solution.py:641
  37.9 0.6 %copy.17 = bf16[2,4,512]{2,1,0:T(4,128)(2,1)} copy(bf16[2,4,512]{2,1,0:T(4,128)(2,1)S(1)} %get-tuple-element.2) | data formatting | bytes 16384
  38.5 0.6 %copy.18 = bf16[2,4,2048]{2,1,0:T(4,128)(2,1)} copy(bf16[2,4,2048]{2,1,0:T(4,128)(2,1)S(1)} %get-tuple-element.3) | data formatting | bytes 65536
